TPU v7x, 32 devices: a whole 2x2x4 slice. The times are simulated.
32 devices in a mesh: leaf: 32 (over z, y, x, core).
Axes of the slice: x: 2, y: 2, z: 4, core: 2. Of those that a mesh axis runs over, the one named last changes fastest.
Arguments:
- points: bfloat16 [64, 131072], P(None, 'leaf'), may hold values from -0.8 to 0.8
- leaf_order: int32 [131072], P('leaf'), may hold values from 0 to 4095, as said below
- near_pairs: int32 [256, 4], P('leaf'), may hold values from -1 to 255, as said below
- solution: float32 [64, 131072], P(None, 'leaf'), may hold values from -6 to 6
- residual: float32 [64, 131072], P(None, 'leaf'), may hold values from -44 to 44
- direction: float32 [64, 131072], P(None, 'leaf'), may hold values from -44 to 44
- skeleton_basis: bfloat16 [256, 131072], P(None, 'leaf'), may hold values from -0.1875 to 0.1875
- transfers: float32 [160, 256, 256], P('leaf'), may hold values from -0.375 to 0.375
- couplings: float32 [6, 256, 256], replicated, may hold values from -0.375 to 0.375
Outputs:
- new_solution: float32 [64, 131072], P(None, 'leaf')
- new_residual: float32 [64, 131072], P(None, 'leaf')
- new_direction: float32 [64, 131072], P(None, 'leaf')
Inputs may be any that keep to these rules, and one draw needn't show every extreme that they name: `leaf_order`: the entries of each slab's 4096 positions are a permutation of 0 to 4095. `near_pairs`: row a lists 4 different later leaves: the first is always a + 1, the others lie among a + 2 to a + 8; -1 stands where that leaf would lie past the last leaf.
All inputs are finite; a program needn't handle non-finite values.
Results may differ from a plain program's by a relative error of at most 0.0034.
The roundings to bfloat16 on the way count: a program that leaves them out, or rounds other values in their place, can miss the bound.
Values may be sent and summed in bfloat16 or wider, within the bound.
A program may use at most 128 MiB of HBM per device.

v0:
```python
import jax
import jax.numpy as jnp
from jax import lax
from jax.sharding import PartitionSpec as P

SHARPNESS = 2.0
EPSILON = 1e-06
HIGHEST = lax.Precision.HIGHEST


def swapped(block, axis, apart):
    count = lax.axis_size(axis)
    route = []
    for low in range(count):
        high = low | 1 << apart
        if high != low and high < count:
            route += [(low, high), (high, low)]
    return lax.ppermute(block, axis, route)


def passed_along(x, axis, by):
    peers = lax.axis_size(axis)
    pairs = [(i, i + by) for i in range(peers) if 0 <= i + by < peers]
    return lax.ppermute(x, axis, pairs)


def couple(level_total, weights):
    halfway = jnp.dot(level_total, weights, precision=HIGHEST)
    return lax.dot_general(halfway, weights, (((1,), (1,)), ((), ())), precision=HIGHEST)


def leaf_terms(win_pts, win_vec, win_sq, sources, others, src_weight, other_weight):

    def per_leaf(pieces):
        source, partner, weight_src, weight_oth = pieces
        source_pts = lax.dynamic_index_in_dim(win_pts, source, 1, keepdims=False)
        source_sq = lax.dynamic_index_in_dim(win_sq, source, 0, keepdims=False)
        source_val = lax.dynamic_index_in_dim(win_vec, source, 1, keepdims=False)
        partner_pts = jnp.take(win_pts, partner, axis=1)
        partner_sq = jnp.take(win_sq, partner, axis=0)
        cross_dot = jnp.einsum(
            "dk,dnj->nkj", source_pts, partner_pts, preferred_element_type=jnp.float32
        )
        distance = source_sq[None, :, None] + partner_sq[:, None, :] - 2.0 * cross_dot
        kernel_tile = jnp.exp(-SHARPNESS * distance).astype(jnp.bfloat16)
        to_partner = (
            jnp.einsum("nkj,rk->nrj", kernel_tile, source_val, preferred_element_type=jnp.float32)
            * weight_oth[:, None, None]
        )
        partner_val = jnp.take(win_vec, partner, axis=1)
        to_source = jnp.einsum(
            "nkj,rnj->nrk", kernel_tile, partner_val, preferred_element_type=jnp.float32
        )
        to_source = jnp.sum(to_source * weight_src[:, None, None], axis=0)
        return (to_source, to_partner)

    return lax.map(per_leaf, (sources, others, src_weight, other_weight))


def spread_rows(targets, contribs, slot_count):
    onehot = (targets[..., None] == jnp.arange(slot_count, dtype=jnp.int32)).astype(jnp.float32)
    return jnp.einsum("anw,anrj->rwj", onehot, contribs, precision=HIGHEST)


def local(
    points,
    leaf_order,
    near_pairs,
    solution,
    residual,
    direction,
    skeleton_basis,
    transfers,
    couplings,
):
    tree_depth = transfers.shape[0]
    leaf_count = near_pairs.shape[0]
    coord_count = points.shape[0]
    rhs_count = direction.shape[0]
    slab_points = points.shape[1]
    leaf_size = slab_points // leaf_count
    first_leaf = lax.axis_index("leaf") * leaf_count
    has_prior = lax.axis_index("leaf") > 0
    tree_points = jnp.take(points, leaf_order, axis=1)
    p_half = direction.astype(jnp.bfloat16)
    stacked = jnp.concatenate([tree_points, p_half], axis=0)
    level_skel = jnp.einsum("ri,ci->rc", p_half, skeleton_basis, preferred_element_type=jnp.float32)
    skeletons = [level_skel]
    for level_idx in range(tree_depth):
        level_skel = jnp.dot(level_skel, transfers[level_idx], precision=HIGHEST)
        skeletons.append(level_skel)
    local_norm = jnp.sum(residual * residual, axis=1)
    top_total, old_norm = lax.psum((skeletons[tree_depth], local_norm), "leaf")
    running = jnp.stack(skeletons[:tree_depth])
    totals = []
    for level_bit in range(tree_depth):
        running = running + swapped(running, "leaf", level_bit)
        totals.append(running[0])
        running = running[1:]
    descent = couple(top_total, couplings[tree_depth])
    for level_idx in reversed(range(tree_depth)):
        descent = lax.dot_general(
            descent, transfers[level_idx], (((1,), (1,)), ((), ())), precision=HIGHEST
        ) + couple(totals[level_idx], couplings[level_idx])
    far = jnp.dot(descent.astype(jnp.bfloat16), skeleton_basis, preferred_element_type=jnp.float32)
    local_valid = near_pairs >= 0
    prior_lists = passed_along(near_pairs, "leaf", 1)
    prior_valid = (prior_lists >= 0) & has_prior
    own_slots = first_leaf + jnp.arange(leaf_count, dtype=jnp.int32)
    incoming = jnp.sum(
        ((near_pairs[..., None] == own_slots) & local_valid[..., None]).astype(jnp.int32),
        axis=(0, 1),
    )
    incoming = incoming + jnp.sum(
        ((prior_lists[..., None] == own_slots) & prior_valid[..., None]).astype(jnp.int32),
        axis=(0, 1),
    )
    pair_totals = jnp.sum(local_valid.astype(jnp.int32), axis=1) + incoming
    self_weight = (1 + pair_totals).astype(jnp.float32)
    valid_float = local_valid.astype(jnp.float32)
    own_index = jnp.arange(leaf_count, dtype=jnp.int32)
    ahead = passed_along(stacked, "leaf", -1)
    window = jnp.concatenate([stacked, ahead], axis=1)
    slot_count = window.shape[1] // leaf_size
    window = window.reshape(coord_count + rhs_count, slot_count, leaf_size)
    win_pts = window[:coord_count]
    win_vec = window[coord_count:]
    win_sq = jnp.sum(jnp.square(win_pts.astype(jnp.float32)), axis=0)
    partner_slots = jnp.where(local_valid, near_pairs - first_leaf, own_index[:, None])
    others = jnp.concatenate([own_index[:, None], partner_slots], axis=1)
    src_weight = jnp.concatenate([self_weight[:, None], valid_float], axis=1)
    zero_column = jnp.zeros((leaf_count, 1), jnp.float32)
    other_weight = jnp.concatenate([zero_column, valid_float], axis=1)
    to_source, to_partner = leaf_terms(
        win_pts, win_vec, win_sq, own_index, others, src_weight, other_weight
    )
    window_sum = spread_rows(others, to_partner, slot_count) + spread_rows(
        own_index[:, None], to_source[:, None], slot_count
    )
    near_local = window_sum[:, :leaf_count].reshape(rhs_count, slab_points)
    outgoing = window_sum[:, leaf_count:].reshape(rhs_count, slab_points)
    near = near_local + passed_along(outgoing.astype(jnp.bfloat16), "leaf", 1).astype(
        outgoing.dtype
    )
    image = direction + near + far
    curve_sum = lax.psum(jnp.sum(direction * image, axis=1), "leaf")
    step_size = old_norm / (curve_sum + EPSILON)
    new_residual = residual - step_size[:, None] * image
    new_norm = lax.psum(jnp.sum(new_residual * new_residual, axis=1), "leaf")
    new_solution = solution + step_size[:, None] * direction
    ratio = new_norm / (old_norm + EPSILON)
    new_direction = new_residual + ratio[:, None] * direction
    return (new_solution, new_residual, new_direction)


def solution(mesh):
    in_specs = (
        P(None, "leaf"),
        P("leaf"),
        P("leaf", None),
        P(None, "leaf"),
        P(None, "leaf"),
        P(None, "leaf"),
        P(None, "leaf"),
        P("leaf", None, None),
        P(),
    )
    out_specs = (P(None, "leaf"), P(None, "leaf"), P(None, "leaf"))
    return jax.shard_map(local, mesh=mesh, in_specs=in_specs, out_specs=out_specs, check_vma=False)
```

profile of v0, /device:TPU:0, one launch (start us, length us, event | category | flops | bytes accessed | tf_op | source)
XLA Modules:
  0.0 528.4 jit_solution(16653307643578137582)
XLA Ops:
  8.1 2.3 collective-permute-start.1
  15.8 2.7 collective-permute-start.3
  20.1 15.0 %gather_fusion.3 = bf16[4096,64]{1,0:T(8,128)(2,1)} fusion(bf16[64,4096]{0,1:T(8,128)(2,1)S(1)} %copy.30, s32[4096]{0:T(1024)S(1)} %fusion.91), kind=kCustom, calls=%fused_computation.3 | custom fusion | bytes 1064960 | tf_op jit(solution)/shard_map/jit(_take)/gather | solution.py:84
  35.1 3.5 select_bitcast_fusion
  44.7 95.9 %all-reduce.4.cloned.1.call-done = f32[64,256]{1,0:T(8,128)} async-done(((f32[64,256]{1,0:T(8,128)}), f32[64,256]{1,0:T(8,128)}) %all-reduce.4.cloned.1.call-update) | async-done | bytes 65552 | tf_op jit(solution)/shard_map/psum | solution.py:93
  147.4 5.6 %collective-permute-done.4 = f32[4,64,256]{2,1,0:T(8,128)S(1)} collective-permute-done((f32[4,64,256]{2,1,0:T(8,128)S(1)}, f32[4,64,256]{2,1,0:T(8,128)S(1)}, u32[]{:S(2)}, u32[]{:S(2)}) %collective-permute-start.4) | collective-permute-done | bytes 262176 | tf_op jit(solution)/shard_map/ppermute | solution.py:18
  154.9 5.5 %collective-permute-done.5 = f32[3,64,256]{2,1,0:T(8,128)S(1)} collective-permute-done((f32[3,64,256]{2,1,0:T(8,128)S(1)}, f32[3,64,256]{2,1,0:T(8,128)S(1)}, u32[]{:S(2)}, u32[]{:S(2)}) %collective-permute-start.5) | collective-permute-done | bytes 196640 | tf_op jit(solution)/shard_map/ppermute | solution.py:18
  160.8 4.8 collective-permute-done.6
  166.8 4.4 collective-permute-done.7
  173.7 1.8 pad_maximum_fusion
  176.7 2.7 fusion.97
  179.5 2.9 copy.38
  182.3 2.7 copy.37
  185.0 230.2 %while.12 = (s32[]{:T(128)}, f32[8,64,512]{2,0,1:T(8,128)}, f32[8,5,64,512]{3,0,1,2:T(8,128)}, s32[8,5]{1,0:T(8,128)S(1)}, bf16[64,16,512]{2,0,1:T(8,128)(2,1)},...) while((s32[]{:T(128)}, f32[8,64,512]{2,0,1:T(8,128)}, ...), condition=%wide.region_8.10_spmd, body=%wide.region_6.0_spmd.sunk | while | flops 510661184 | bytes 13959699 | solution.py:57
  190.3 1.8 gather_fusion.1
  192.1 2.6 fusion.142
  197.9 3.7 dynamic_update_slice.10
  201.7 12.1 %dynamic_update_slice.11 = f32[8,5,64,512]{3,0,1,2:T(8,128)} dynamic-update-slice(f32[8,5,64,512]{3,0,1,2:T(8,128)} %get-tuple-element.212, f32[1,5,64,512]{3,0,1,2:T(1,128)S(1)} %copy.59, s32[]{:T(128)S(6)} %copy.65, s32[]{:T(128)} %constant.56.clone.1..sunk, s32[]{:T(128)} %constant.56.clone.1..sunk, s32[]{:T(128)} %constant.56.clone.1..sunk) | dynamic-update-slice | bytes 1310724 | tf_op jit(solution)/shard_map/while/body/jit(dynamic_update_index_in_dim)/dynamic_update_slice | solution.py:57
  219.0 1.8 gather_fusion.1
  220.8 2.6 fusion.142
  226.7 3.7 dynamic_update_slice.10
  230.4 12.1 %dynamic_update_slice.11 = f32[8,5,64,512]{3,0,1,2:T(8,128)} dynamic-update-slice(f32[8,5,64,512]{3,0,1,2:T(8,128)} %get-tuple-element.212, f32[1,5,64,512]{3,0,1,2:T(1,128)S(1)} %copy.59, s32[]{:T(128)S(6)} %copy.65, s32[]{:T(128)} %constant.56.clone.1..sunk, s32[]{:T(128)} %constant.56.clone.1..sunk, s32[]{:T(128)} %constant.56.clone.1..sunk) | dynamic-update-slice | bytes 1310724 | tf_op jit(solution)/shard_map/while/body/jit(dynamic_update_index_in_dim)/dynamic_update_slice | solution.py:57
  249.6 2.6 fusion.142
  255.5 3.7 dynamic_update_slice.10
  259.2 12.1 %dynamic_update_slice.11 = f32[8,5,64,512]{3,0,1,2:T(8,128)} dynamic-update-slice(f32[8,5,64,512]{3,0,1,2:T(8,128)} %get-tuple-element.212, f32[1,5,64,512]{3,0,1,2:T(1,128)S(1)} %copy.59, s32[]{:T(128)S(6)} %copy.65, s32[]{:T(128)} %constant.56.clone.1..sunk, s32[]{:T(128)} %constant.56.clone.1..sunk, s32[]{:T(128)} %constant.56.clone.1..sunk) | dynamic-update-slice | bytes 1310724 | tf_op jit(solution)/shard_map/while/body/jit(dynamic_update_index_in_dim)/dynamic_update_slice | solution.py:57
  278.4 2.6 fusion.142
  284.2 3.7 dynamic_update_slice.10
  288.0 12.1 %dynamic_update_slice.11 = f32[8,5,64,512]{3,0,1,2:T(8,128)} dynamic-update-slice(f32[8,5,64,512]{3,0,1,2:T(8,128)} %get-tuple-element.212, f32[1,5,64,512]{3,0,1,2:T(1,128)S(1)} %copy.59, s32[]{:T(128)S(6)} %copy.65, s32[]{:T(128)} %constant.56.clone.1..sunk, s32[]{:T(128)} %constant.56.clone.1..sunk, s32[]{:T(128)} %constant.56.clone.1..sunk) | dynamic-update-slice | bytes 1310724 | tf_op jit(solution)/shard_map/while/body/jit(dynamic_update_index_in_dim)/dynamic_update_slice | solution.py:57
  305.4 1.8 gather_fusion.1
  307.2 2.6 fusion.142
  313.0 3.7 dynamic_update_slice.10
  316.8 12.1 %dynamic_update_slice.11 = f32[8,5,64,512]{3,0,1,2:T(8,128)} dynamic-update-slice(f32[8,5,64,512]{3,0,1,2:T(8,128)} %get-tuple-element.212, f32[1,5,64,512]{3,0,1,2:T(1,128)S(1)} %copy.59, s32[]{:T(128)S(6)} %copy.65, s32[]{:T(128)} %constant.56.clone.1..sunk, s32[]{:T(128)} %constant.56.clone.1..sunk, s32[]{:T(128)} %constant.56.clone.1..sunk) | dynamic-update-slice | bytes 1310724 | tf_op jit(solution)/shard_map/while/body/jit(dynamic_update_index_in_dim)/dynamic_update_slice | solution.py:57
  334.1 1.8 gather_fusion.1
  335.9 2.6 fusion.142
  341.8 3.7 dynamic_update_slice.10
  345.5 12.1 %dynamic_update_slice.11 = f32[8,5,64,512]{3,0,1,2:T(8,128)} dynamic-update-slice(f32[8,5,64,512]{3,0,1,2:T(8,128)} %get-tuple-element.212, f32[1,5,64,512]{3,0,1,2:T(1,128)S(1)} %copy.59, s32[]{:T(128)S(6)} %copy.65, s32[]{:T(128)} %constant.56.clone.1..sunk, s32[]{:T(128)} %constant.56.clone.1..sunk, s32[]{:T(128)} %constant.56.clone.1..sunk) | dynamic-update-slice | bytes 1310724 | tf_op jit(solution)/shard_map/while/body/jit(dynamic_update_index_in_dim)/dynamic_update_slice | solution.py:57
  364.7 2.6 fusion.142
  370.6 3.7 dynamic_update_slice.10
  374.3 12.1 %dynamic_update_slice.11 = f32[8,5,64,512]{3,0,1,2:T(8,128)} dynamic-update-slice(f32[8,5,64,512]{3,0,1,2:T(8,128)} %get-tuple-element.212, f32[1,5,64,512]{3,0,1,2:T(1,128)S(1)} %copy.59, s32[]{:T(128)S(6)} %copy.65, s32[]{:T(128)} %constant.56.clone.1..sunk, s32[]{:T(128)} %constant.56.clone.1..sunk, s32[]{:T(128)} %constant.56.clone.1..sunk) | dynamic-update-slice | bytes 1310724 | tf_op jit(solution)/shard_map/while/body/jit(dynamic_update_index_in_dim)/dynamic_update_slice | solution.py:57
  393.5 2.6 fusion.142
  399.3 3.7 dynamic_update_slice.10
  403.1 12.1 %dynamic_update_slice.11 = f32[8,5,64,512]{3,0,1,2:T(8,128)} dynamic-update-slice(f32[8,5,64,512]{3,0,1,2:T(8,128)} %get-tuple-element.212, f32[1,5,64,512]{3,0,1,2:T(1,128)S(1)} %copy.59, s32[]{:T(128)S(6)} %copy.65, s32[]{:T(128)} %constant.56.clone.1..sunk, s32[]{:T(128)} %constant.56.clone.1..sunk, s32[]{:T(128)} %constant.56.clone.1..sunk) | dynamic-update-slice | bytes 1310724 | tf_op jit(solution)/shard_map/while/body/jit(dynamic_update_index_in_dim)/dynamic_update_slice | solution.py:57
  415.2 2.4 fusion.94
  417.6 4.8 fusion.24
  430.9 43.4 %all-reduce.1 = (f32[64]{0:T(128)S(1)}, f32[64]{0:T(128)S(1)}) all-reduce(f32[64]{0:T(128)S(1)} %multiply_reduce_fusion.3, f32[64]{0:T(128)S(1)} %get-tuple-element.126), channel_id=1, replica_groups=mesh['leaf'=32] {'leaf'}, use_global_device_ids=true, to_apply=%region_1.2 | all-reduce | flops 128 | bytes 1024 | tf_op jit(solution)/shard_map/psum | solution.py:93
  474.3 4.2 multiply_reduce_fusion.1
  478.5 40.7 %psum.31 = f32[64]{0:T(128)S(1)} all-reduce(f32[64]{0:T(128)S(1)} %get-tuple-element.105), channel_id=1, replica_groups=mesh['leaf'=32] {'leaf'}, use_global_device_ids=true, to_apply=%region_13.15 | all-reduce | flops 64 | bytes 512 | tf_op jit(solution)/shard_map/psum | solution.py:149
  519.2 2.4 multiply_add_fusion
  (219 shorter events, 93.9 us)
Async XLA Ops:
  7.2 5.0 copy-start
  7.2 133.4 %all-reduce.4.cloned.1.call-start = ((), (), s32[]{:S(2)}) async-start(), calls=%async_computation | async-start | bytes 131072 | tf_op jit(solution)/shard_map/psum | solution.py:93
  8.1 36.1 %collective-permute-start.1 = (s32[8,4]{1,0:T(8,128)S(1)}, s32[8,4]{1,0:T(8,128)S(1)}, u32[]{:S(2)}, u32[]{:S(2)}) collective-permute-start(s32[8,4]{1,0:T(8,128)S(1)} %copy.28), channel_id=1, source_target_pairs={{0,1},{1,2},{2,3},{3,4},{4,5},{5,6},{6,7},{7,8},{8,9},{9,10},{10,1... | collective-permute-start | bytes 392 | tf_op jit(solution)/shard_map/ppermute | solution.py:24
  12.2 2.2 copy-start.1
  12.2 1.7 copy-start.8
  12.2 6.3 %copy-start.11 = (s32[4096]{0:T(1024)S(1)}, s32[4096]{0:T(1024)}, u32[]{:S(2)}) copy-start(s32[4096]{0:T(1024)} %param.14) | copy-start | bytes 49156
  15.8 127.5 %collective-permute-start.3 = (f32[5,64,256]{2,1,0:T(8,128)S(1)}, f32[5,64,256]{2,1,0:T(8,128)}, u32[]{:S(2)}, u32[]{:S(2)}) collective-permute-start(f32[5,64,256]{2,1,0:T(8,128)S(1)} %get-tuple-element.124), channel_id=1, source_target_pairs={{0,1},{1,0},{2,3},{3,2},{4,5},{5,4},{6,7},{7,6},{8,9},{9,8},{10,11... | collective-permute-start | bytes 983048 | tf_op jit(solution)/shard_map/ppermute | solution.py:18
  35.1 4.4 copy-start.2
  38.6 1.0 copy-start.4
  39.5 4.8 copy-start.12
  41.1 132.6 %collective-permute-start = (bf16[128,4096]{0,1:T(8,128)(2,1)}, bf16[128,4096]{0,1:T(8,128)(2,1)}, u32[]{:S(2)}, u32[]{:S(2)}) collective-permute-start(bf16[128,4096]{0,1:T(8,128)(2,1)} %pad_maximum_fusion.1), channel_id=1, source_target_pairs={{1,0},{2,1},{3,2},{4,3},{5,4},{6,5},{7,6},{8,7},{9,8},{10,9},{11,1... | collective-permute-start | bytes 3145736 | tf_op jit(solution)/shard_map/ppermute | solution.py:24
  140.6 6.6 %copy-start.7 = (f32[6,256,256]{2,1,0:T(8,128)S(1)}, f32[6,256,256]{2,1,0:T(8,128)}, u32[]{:S(2)}) copy-start(f32[6,256,256]{2,1,0:T(8,128)} %param.21) | copy-start | bytes 4718596
  144.3 8.7 %collective-permute-start.4 = (f32[4,64,256]{2,1,0:T(8,128)S(1)}, f32[4,64,256]{2,1,0:T(8,128)S(1)}, u32[]{:S(2)}, u32[]{:S(2)}) collective-permute-start(f32[4,64,256]{2,1,0:T(8,128)S(1)} %slice.118), channel_id=1, source_target_pairs={{0,2},{2,0},{1,3},{3,1},{4,6},{6,4},{5,7},{7,5},{8,10},{10,8},{9,1... | collective-permute-start | bytes 786440 | tf_op jit(solution)/shard_map/ppermute | solution.py:18
  153.0 18.8 %copy-start.9 = (f32[5,256,256]{2,1,0:T(8,128)S(1)}, f32[5,256,256]{2,1,0:T(8,128)}, u32[]{:S(2)}) copy-start(f32[5,256,256]{2,1,0:T(8,128)} %param.20) | copy-start | bytes 3932164
  153.1 7.3 %collective-permute-start.5 = (f32[3,64,256]{2,1,0:T(8,128)S(1)}, f32[3,64,256]{2,1,0:T(8,128)S(1)}, u32[]{:S(2)}, u32[]{:S(2)}) collective-permute-start(f32[3,64,256]{2,1,0:T(8,128)S(1)} %slice.119), channel_id=1, source_target_pairs={{0,4},{4,0},{1,5},{5,1},{2,6},{6,2},{3,7},{7,3},{8,12},{12,8},{9,1... | collective-permute-start | bytes 589832 | tf_op jit(solution)/shard_map/ppermute | solution.py:18
  160.4 13.3 %copy-start.5 = (bf16[64,4096]{0,1:T(8,128)(2,1)S(1)}, bf16[64,4096]{0,1:T(8,128)(2,1)}, u32[]{:S(2)}) copy-start(bf16[64,4096]{0,1:T(8,128)(2,1)} %copy-done.4) | copy-start | bytes 1572868
  160.4 5.1 collective-permute-start.6
  165.6 5.7 %collective-permute-start.7 = (f32[1,64,256]{2,1,0:T(8,128)S(1)}, f32[1,64,256]{2,1,0:T(8,128)S(1)}, u32[]{:S(2)}, u32[]{:S(2)}) collective-permute-start(f32[1,64,256]{2,1,0:T(8,128)S(1)} %slice.121), channel_id=1, source_target_pairs={{0,16},{16,0},{1,17},{17,1},{2,18},{18,2},{3,19},{19,3},{4,20},{20... | collective-permute-start | bytes 196616 | tf_op jit(solution)/shard_map/ppermute | solution.py:18
  422.6 6.0 %collective-permute-start.2 = (bf16[64,4096]{1,0:T(8,128)(2,1)S(1)}, bf16[64,4096]{1,0:T(8,128)(2,1)S(1)}, u32[]{:S(2)}, u32[]{:S(2)}) collective-permute-start(bf16[64,4096]{1,0:T(8,128)(2,1)S(1)} %bitcast.211), channel_id=1, source_target_pairs={{0,1},{1,2},{2,3},{3,4},{4,5},{5,6},{6,7},{7,8},{8,9},{9,10},{10,1... | collective-permute-start | bytes 1572872 | tf_op jit(solution)/shard_map/ppermute | solution.py:24
  427.9 1.2 copy-start.3
  428.6 2.2 copy-start.6
  428.7 2.2 copy-start.10
Sparse Core Ops, SparseCore 0:
  15.9 124.6 all-reduce.3
where the time goes:
time: 534 us; the launch traced here: 528 us
  local copies, waits for them, and re-layouts  203 us (38%)
  waiting for transfers between devices  116 us (22%)
  blocking collectives  84.1 us (16%)
  matrix products  62.8 us (12%)
  other arithmetic  18.4 us (3%)
  loops' own time  17.3 us (3%)
  between operations  14.5 us (3%)
  starting transfers between devices  11.8 us (2%)
    dynamic_update_slice x32, local copies, waits for them, and re-layouts, leaf_terms(): return lax.map(per_leaf, (sources, others, src_weight, other_weight))  133 us
    psum x1, waiting for transfers between devices, local(): top_total, old_norm = lax.psum((skeletons[tree_depth], local_norm), 'leaf')  95.9 us
    psum x1, blocking collectives, local(): top_total, old_norm = lax.psum((skeletons[tree_depth], local_norm), 'leaf')  43.4 us
    psum x1, blocking collectives, local(): new_norm = lax.psum(jnp.sum(new_residual * new_residual, axis=1), 'leaf')  40.7 us
    dot_general x8, matrix products, per_leaf(): jnp.einsum('dk,dnj->nkj', source_pts, partner_pts, preferred_element_type...  21 us
    ppermute x5, waiting for transfers between devices, swapped(): return lax.ppermute(block, axis, route)  20.3 us
    another operation x1, loops' own time, leaf_terms(): return lax.map(per_leaf, (sources, others, src_weight, other_weight))  17.3 us
    gather x1, local copies, waits for them, and re-layouts, local(): tree_points = jnp.take(points, leaf_order, axis=1)  15 us
  transfers between devices with their start and end apart: 9, of which 5 were waited for; matrix products, arithmetic and copies ran while one was open for 8% of the time, Pallas kernels for 0%

commit v1 on v0

v1 whole, which is shorter than its diff:
```python
import functools
import math

import jax
import jax.numpy as jnp
from jax import lax
from jax.experimental import pallas as pl
from jax.experimental.pallas import tpu as pltpu
from jax.sharding import PartitionSpec as P

SHARPNESS = 2.0
EPSILON = 1e-06
HIGHEST = lax.Precision.HIGHEST
MESH = pl.DeviceIdType.MESH
LANES = 128
EXTRA = 16
GROUP = 8
VMEM_LIMIT = 56 * 1024 * 1024
NT = (((1,), (1,)), ((), ()))


def shifted(x, axis, by, wrap=False):
    peers = lax.axis_size(axis)
    pairs = [(i, (i + by) % peers) for i in range(peers) if wrap or 0 <= i + by < peers]
    return lax.ppermute(x, axis, pairs)


def swapped(x, axis, bit):
    count = lax.axis_size(axis)
    return lax.ppermute(x, axis, [(i, i ^ (1 << bit)) for i in range(count)])


def arrange_kernel(points_ref, order_ref, direction_ref, stack_ref, turned_ref, tall):
    coords, slab = points_ref.shape
    width = order_ref.shape[1]
    chunks = slab // LANES

    @pl.when(pl.program_id(0) == 0)
    def _():
        for h in range(chunks):
            tall[h * coords : (h + 1) * coords, :] = points_ref[:, h * LANES : (h + 1) * LANES]

    order = order_ref[...]
    high = order // LANES
    low = order - high * LANES
    rows = lax.broadcasted_iota(jnp.int32, (LANES, width), 0)
    onehot = jnp.where(rows == low, 1.0, 0.0).astype(jnp.bfloat16)
    picked = jnp.zeros((coords, width), jnp.float32)
    step = 4
    for c in range(0, chunks, step):
        part = jnp.dot(
            tall[c * coords : (c + step) * coords, :], onehot, preferred_element_type=jnp.float32
        )
        for h in range(step):
            picked = jnp.where(high == c + h, part[h * coords : (h + 1) * coords], picked)
    half = -0.5 * jnp.sum(picked * picked, axis=0, keepdims=True)
    first = half.astype(jnp.bfloat16).astype(jnp.float32)
    second = (half - first).astype(jnp.bfloat16).astype(jnp.float32)
    third = (half - first - second).astype(jnp.bfloat16).astype(jnp.float32)

    def extra(height, at_parts, at_ones):
        row = lax.broadcasted_iota(jnp.int32, (height, width), 0)
        out = jnp.where((row >= at_ones) & (row < at_ones + 3), 1.0, 0.0)
        for i, piece in enumerate((first, second, third)):
            out = jnp.where(row == at_parts + i, piece, out)
        return out

    stack_ref[0:coords, :] = picked.astype(jnp.bfloat16)
    stack_ref[coords : coords + EXTRA, :] = extra(EXTRA, 0, 3).astype(jnp.bfloat16)
    stack_ref[coords + EXTRA :, :] = direction_ref[...].astype(jnp.bfloat16)
    wide = jnp.concatenate([picked, extra(LANES - coords, 3, 0)], axis=0)
    turned_ref[...] = wide.T.astype(jnp.bfloat16)


def arrange(points, leaf_order, direction, leaf_size):
    coords, slab = points.shape
    rhs = direction.shape[0]
    height = coords + EXTRA + rhs
    return pl.pallas_call(
        arrange_kernel,
        grid=(slab // leaf_size,),
        in_specs=[
            pl.BlockSpec((coords, slab), lambda j: (0, 0)),
            pl.BlockSpec((1, leaf_size), lambda j: (0, j)),
            pl.BlockSpec((rhs, leaf_size), lambda j: (0, j)),
        ],
        out_specs=[
            pl.BlockSpec((height, leaf_size), lambda j: (0, j)),
            pl.BlockSpec((leaf_size, LANES), lambda j: (j, 0)),
        ],
        out_shape=[
            jax.ShapeDtypeStruct((height, slab), jnp.bfloat16),
            jax.ShapeDtypeStruct((slab, LANES), jnp.bfloat16),
        ],
        scratch_shapes=[pltpu.VMEM((slab // LANES * coords, LANES), jnp.bfloat16)],
        compiler_params=pltpu.CompilerParams(vmem_limit_bytes=VMEM_LIMIT),
        cost_estimate=pl.CostEstimate(
            flops=2 * coords * slab * slab, bytes_accessed=5 << 20, transcendentals=0
        ),
        name="arrange",
    )(points, leaf_order.reshape(1, slab), direction)


def rise_kernel(direction_ref, basis_ref, transfers_ref, skel_ref):
    value = lax.dot_general(
        direction_ref[...].astype(jnp.bfloat16),
        basis_ref[...],
        NT,
        preferred_element_type=jnp.float32,
    )
    skel_ref[0] = value
    for k in range(transfers_ref.shape[0]):
        value = jnp.dot(
            value, transfers_ref[k], precision=HIGHEST, preferred_element_type=jnp.float32
        )
        skel_ref[k + 1] = value


def rise(direction, basis, transfers):
    rhs = direction.shape[0]
    depth, rank = transfers.shape[:2]
    return pl.pallas_call(
        rise_kernel,
        out_shape=jax.ShapeDtypeStruct((depth + 1, rhs, rank), jnp.float32),
        compiler_params=pltpu.CompilerParams(vmem_limit_bytes=VMEM_LIMIT),
        cost_estimate=pl.CostEstimate(
            flops=2 * rhs * rank * (basis.shape[1] + 6 * depth * rank),
            bytes_accessed=5 << 20,
            transcendentals=0,
        ),
        name="rise",
    )(direction, basis, transfers)


def near_kernel(crossing, coords, rhs, *refs):
    if crossing:
        (lists, before, first_ref, turned, own, ahead, behind, start, out, acc) = refs
    else:
        (lists, before, first_ref, turned, own, out, acc) = refs
    leaves, partners = lists.shape
    leaf = turned.shape[0] // leaves
    deep = coords + EXTRA
    scale = 2.0 * SHARPNESS * math.log2(math.e)
    first = first_ref[0]
    target = pl.program_id(0)
    mine = pl.multiple_of(target * leaf, leaf)

    def product(ref, slot):
        cols = pl.ds(pl.multiple_of(slot * leaf, leaf), leaf)
        exponent = jnp.dot(
            turned[pl.ds(mine, leaf), 0:deep],
            ref[0:deep, cols],
            preferred_element_type=jnp.float32,
        )
        tile = jnp.exp2(exponent * scale).astype(jnp.bfloat16)
        return lax.dot_general(tile, ref[deep:, cols], NT, preferred_element_type=jnp.float32)

    def lists_me(ref, row):
        found = ref[row, 0] == first + target
        for m in range(1, partners):
            found = found | (ref[row, m] == first + target)
        return found

    if crossing:
        acc[...] = jnp.zeros_like(acc)
    else:
        count = jnp.int32(1)
        for m in range(partners):
            count += jnp.where(lists[target, m] >= 0, 1, 0)
        for a in range(leaves):
            count += jnp.where(lists_me(lists, a), 1, 0)
            count += jnp.where(lists_me(before, a), 1, 0)
        acc[...] = product(own, target) * count.astype(jnp.float32)

    def forward(m, carry):
        slot = lists[target, m] - first
        known = lists[target, m] >= 0
        if crossing:

            @pl.when(known & (slot >= leaves))
            def _():
                acc[...] += product(ahead, slot - leaves)
        else:

            @pl.when(known & (slot < leaves))
            def _():
                acc[...] += product(own, slot)

        return carry

    def backward(a, carry):
        @pl.when(lists_me(before if crossing else lists, a))
        def _():
            acc[...] += product(behind if crossing else own, a)

        return carry

    lax.fori_loop(0, partners, forward, 0)
    if crossing:
        lax.fori_loop(target, leaves, backward, 0)
        out[...] = acc[...].T + start[...]
    else:
        lax.fori_loop(0, target, backward, 0)
        out[...] = acc[...].T


def near_terms(crossing, lists, before, first, turned, own, coords, ahead=None, behind=None, start=None):
    leaves = lists.shape[0]
    height, slab = own.shape
    rhs = height - coords - EXTRA
    leaf = slab // leaves
    smem = pl.BlockSpec(memory_space=pltpu.SMEM)
    vmem = pl.BlockSpec(memory_space=pltpu.VMEM)
    block = pl.BlockSpec((rhs, leaf), lambda j: (0, j))
    args = [lists, before, first, turned, own]
    specs = [smem, smem, smem, vmem, vmem]
    if crossing:
        args += [ahead, behind, start]
        specs += [vmem, vmem, block]
    tiles = 5 * leaves
    return pl.pallas_call(
        functools.partial(near_kernel, crossing, coords, rhs),
        grid=(leaves,),
        in_specs=specs,
        out_specs=block,
        out_shape=jax.ShapeDtypeStruct((rhs, slab), jnp.float32),
        scratch_shapes=[pltpu.VMEM((leaf, rhs), jnp.float32)],
        compiler_params=pltpu.CompilerParams(vmem_limit_bytes=VMEM_LIMIT),
        cost_estimate=pl.CostEstimate(
            flops=tiles * 8 * leaf * leaf * LANES,
            bytes_accessed=4 << 20,
            transcendentals=tiles * leaf * leaf,
        ),
        name="near_crossing" if crossing else "near_own",
    )(*args)


def image_kernel(
    count, totals_ref, transfers_ref, couplings_ref, basis_ref, direction_ref, residual_ref,
    near_ref, image_ref, factors_ref, tall, inner, outer, send_in, recv_in, send_out, recv_out,
):
    me = lax.axis_index("leaf")
    groups = count // GROUP
    base = (me // GROUP) * GROUP
    in_peers = [base + (me - base + d) % GROUP for d in range(1, GROUP)]
    out_peers = [(me + GROUP * e) % count for e in range(1, groups)]
    barrier = pltpu.get_barrier_semaphore()
    for peer in in_peers + out_peers:
        pl.semaphore_signal(barrier, inc=1, device_id=(peer,), device_id_type=MESH)

    depth = transfers_ref.shape[0]
    rhs = direction_ref.shape[0]

    def couple(k):
        halfway = jnp.dot(
            totals_ref[k], couplings_ref[k], precision=HIGHEST, preferred_element_type=jnp.float32
        )
        return lax.dot_general(
            halfway, couplings_ref[k], NT, precision=HIGHEST, preferred_element_type=jnp.float32
        )

    descent = couple(depth)
    for k in reversed(range(depth)):
        descent = lax.dot_general(
            descent, transfers_ref[k], NT, precision=HIGHEST, preferred_element_type=jnp.float32
        ) + couple(k)
    descent = descent.astype(jnp.bfloat16)

    slab = direction_ref.shape[1]
    width = 512

    def block(j, sums):
        cols = pl.ds(pl.multiple_of(j * width, width), width)
        far = jnp.dot(descent, basis_ref[:, cols], preferred_element_type=jnp.float32)
        d = direction_ref[:, cols]
        r = residual_ref[:, cols]
        image = d + near_ref[:, cols] + far
        image_ref[:, cols] = image
        pairs = ((r, r), (d, image), (r, image), (image, image))
        return tuple(
            s + sum((x * y)[:, i : i + LANES] for i in range(0, width, LANES))
            for s, (x, y) in zip(sums, pairs)
        )

    zero = jnp.zeros((rhs, LANES), jnp.float32)
    sums = lax.fori_loop(0, slab // width, block, (zero,) * 4)
    lane = lax.broadcasted_iota(jnp.int32, (rhs, LANES), 1)
    packed = zero
    for i, s in enumerate(sums):
        packed = jnp.where(lane == i, jnp.sum(s, axis=1, keepdims=True), packed)
    tall[...] = jnp.zeros_like(tall)
    tall[0:rhs, :] = packed
    inner[0] = tall[...].T[0:8, :]

    pl.semaphore_wait(barrier, len(in_peers) + len(out_peers))

    def exchange(buffer, peers, send, recv):
        copies = []
        for i, peer in enumerate(peers):
            copy = pltpu.make_async_remote_copy(
                src_ref=buffer.at[0],
                dst_ref=buffer.at[i + 1],
                send_sem=send.at[i],
                recv_sem=recv.at[i],
                device_id=(peer,),
                device_id_type=MESH,
            )
            copy.start()
            copies.append(copy)
        for copy in copies:
            copy.wait()
        total = buffer[0]
        for i in range(len(peers)):
            total = total + buffer[i + 1]
        return total

    total = exchange(inner, in_peers, send_in, recv_in)
    if groups > 1:
        outer[0] = total
        total = exchange(outer, out_peers, send_out, recv_out)
    old = total[0:1]
    step = old / (total[1:2] + EPSILON)
    new = jnp.maximum(old - 2.0 * step * total[2:3] + step * step * total[3:4], 0.0)
    ratio = new / (old + EPSILON)
    row = lax.broadcasted_iota(jnp.int32, (LANES, LANES), 0)
    both = jnp.where(row == 0, step, jnp.where(row == 1, ratio, 0.0))
    factors_ref[...] = both.T[0:rhs, :]


def image_and_factors(totals, transfers, couplings, basis, direction, residual, near):
    count = lax.axis_size("leaf")
    groups = count // GROUP
    rhs, slab = direction.shape
    return pl.pallas_call(
        functools.partial(image_kernel, count),
        out_shape=[
            jax.ShapeDtypeStruct((rhs, slab), jnp.float32),
            jax.ShapeDtypeStruct((rhs, LANES), jnp.float32),
        ],
        scratch_shapes=[
            pltpu.VMEM((LANES, LANES), jnp.float32),
            pltpu.VMEM((GROUP, 8, LANES), jnp.float32),
            pltpu.VMEM((max(groups, 2), 8, LANES), jnp.float32),
            pltpu.SemaphoreType.DMA((GROUP - 1,)),
            pltpu.SemaphoreType.DMA((GROUP - 1,)),
            pltpu.SemaphoreType.DMA((max(groups - 1, 1),)),
            pltpu.SemaphoreType.DMA((max(groups - 1, 1),)),
        ],
        compiler_params=pltpu.CompilerParams(
            vmem_limit_bytes=VMEM_LIMIT, collective_id=0, has_side_effects=True
        ),
        cost_estimate=pl.CostEstimate(
            flops=2 * rhs * slab * basis.shape[0], bytes_accessed=10 << 20, transcendentals=0
        ),
        name="image",
    )(totals, transfers, couplings, basis, direction, residual, near)


def update_kernel(factors, solution, residual, direction, image, new_solution, new_residual, new_direction):
    step = factors[:, 0:1]
    ratio = factors[:, 1:2]
    d = direction[...]
    new_solution[...] = solution[...] + step * d
    r = residual[...] - step * image[...]
    new_residual[...] = r
    new_direction[...] = r + ratio * d


def update(factors, solution, residual, direction, image):
    rhs, slab = direction.shape
    width = slab // 4
    block = pl.BlockSpec((rhs, width), lambda j: (0, j))
    shape = jax.ShapeDtypeStruct((rhs, slab), jnp.float32)
    return pl.pallas_call(
        update_kernel,
        grid=(slab // width,),
        in_specs=[pl.BlockSpec((rhs, LANES), lambda j: (0, 0))] + [block] * 4,
        out_specs=[block] * 3,
        out_shape=[shape] * 3,
        compiler_params=pltpu.CompilerParams(vmem_limit_bytes=VMEM_LIMIT),
        name="update",
    )(factors, solution, residual, direction, image)


def local(
    points, leaf_order, near_pairs, solution, residual, direction, skeleton_basis, transfers, couplings
):
    depth = transfers.shape[0]
    leaves = near_pairs.shape[0]
    coords = points.shape[0]
    leaf = points.shape[1] // leaves
    bits = lax.axis_size("leaf").bit_length() - 1
    first = (lax.axis_index("leaf") * leaves).astype(jnp.int32).reshape(1)
    before = shifted(near_pairs, "leaf", 1, wrap=True)
    running = rise(direction, skeleton_basis, transfers)
    own, turned = arrange(points, leaf_order, direction, leaf)
    ahead = shifted(own, "leaf", -1)
    behind = shifted(own, "leaf", 1)
    totals = []
    for bit in range(bits):
        running = running + swapped(running, "leaf", bit)
        if bit < depth:
            totals.append(running[0])
            running = running[1:]
    totals.append(running[0])
    near = near_terms(False, near_pairs, before, first, turned, own, coords)
    near = near_terms(
        True, near_pairs, before, first, turned, own, coords, ahead, behind, near
    )
    image, factors = image_and_factors(
        jnp.stack(totals), transfers, couplings, skeleton_basis, direction, residual, near
    )
    return tuple(update(factors, solution, residual, direction, image))


def solution(mesh):
    in_specs = (
        P(None, "leaf"),
        P("leaf"),
        P("leaf", None),
        P(None, "leaf"),
        P(None, "leaf"),
        P(None, "leaf"),
        P(None, "leaf"),
        P("leaf", None, None),
        P(),
    )
    out_specs = (P(None, "leaf"), P(None, "leaf"), P(None, "leaf"))
    return jax.shard_map(local, mesh=mesh, in_specs=in_specs, out_specs=out_specs, check_vma=False)
```

time: 534 us -> 132 us (0.25); the launches traced: 528 us -> 132 us
  local copies, waits for them, and re-layouts: 203 us -> 3.54 us
  waiting for transfers between devices: 116 us -> 22.6 us
  blocking collectives: 84.1 us -> 0 us
  Pallas kernels: 0 us -> 80.8 us
  matrix products: 62.8 us -> 0 us
  other arithmetic: 18.4 us -> 0.18 us
  loops' own time: 17.3 us -> 0 us
  between operations: 14.5 us -> 0.78 us
  starting transfers between devices: 11.8 us -> 24.2 us
    dynamic_update_slice x32 -> x0, local copies, waits for them, and re-layouts: 133 us -> none  [leaf_terms(): return lax.map(per_leaf, (sources, others, src_weight, other_weight))]
    psum x1 -> x0, waiting for transfers between devices: 95.9 us -> none  [local(): top_total, old_norm = lax.psum((skeletons[tree_depth], local_norm), 'leaf')]
    psum x2 -> x0, blocking collectives: 84.1 us -> none  [the longest x1 43.4 us: local(): top_total, old_norm = lax.psum((skeletons[tree_depth], local_norm), 'leaf')]
    pallas_call x0 -> x6, Pallas kernels: none -> 80.8 us  [the longest x2 32.5 us: near_terms(): pl.pallas_call(functools.partial(near_kernel, crossing, coords, rhs), gri...]
    dot_general x50 -> x0, matrix products: 62.8 us -> none  [the longest x8 21 us: per_leaf(): jnp.einsum('dk,dnj->nkj', source_pts, partner_pts, preferred_element_type...]
    gather x25 -> x0, local copies, waits for them, and re-layouts: 48.2 us -> none  [the longest x1 15 us: local(): tree_points = jnp.take(points, leaf_order, axis=1)]
    another operation x1 -> x0, loops' own time: 17.3 us -> none  [leaf_terms(): return lax.map(per_leaf, (sources, others, src_weight, other_weight))]
    ppermute x8, starting transfers between devices: 11.7 us -> 24.2 us  [the longest x5 17.8 us: swapped(): return lax.ppermute(x, axis, [(i, i ^ 1 << bit) for i in range(count)])]
  transfers between devices with their start and end apart: 9 -> 8, of which waited for: 5 -> 4; matrix products, arithmetic and copies ran while one was open for 8% -> 0% of each run, Pallas kernels for 0% -> 32%
where the time goes in v1:
time: 132 us
  Pallas kernels  80.8 us (61%)
  starting transfers between devices  24.2 us (18%)
  waiting for transfers between devices  22.6 us (17%)
  local copies, waits for them, and re-layouts  3.54 us (3%)
    pallas_call x2, Pallas kernels, near_terms(): pl.pallas_call(functools.partial(near_kernel, crossing, coords, rhs), gri...  32.5 us
    pallas_call x1, Pallas kernels, image_and_factors(): pl.pallas_call(functools.partial(image_kernel, count), out_shape=[jax.Sha...  28.9 us
    ppermute x5, waiting for transfers between devices, swapped(): return lax.ppermute(x, axis, [(i, i ^ 1 << bit) for i in range(count)])  18.5 us
    ppermute x5, starting transfers between devices, swapped(): return lax.ppermute(x, axis, [(i, i ^ 1 << bit) for i in range(count)])  17.8 us
    pallas_call x1, Pallas kernels, arrange(): pl.pallas_call(arrange_kernel, grid=(slab // leaf_size,), in_specs=[pl.Bl...  9.1 us
    ppermute x3, starting transfers between devices, shifted(): return lax.ppermute(x, axis, pairs)  6.43 us
    pallas_call x1, Pallas kernels, rise(): pl.pallas_call(rise_kernel, out_shape=jax.ShapeDtypeStruct((depth + 1, rh...  5.72 us
    pallas_call x1, Pallas kernels, update(): pl.pallas_call(update_kernel, grid=(slab // width,), in_specs=[pl.BlockSp...  4.49 us
  transfers between devices with their start and end apart: 8, of which 4 were waited for; matrix products, arithmetic and copies ran while one was open for 0% of the time, Pallas kernels for 32%

profile of v1, /device:TPU:0, one launch (start us, length us, event | category | flops | bytes accessed | tf_op | source)
XLA Modules:
  0.0 132.1 jit_solution(11030441804999756686)
XLA Ops:
  0.6 5.7 %rise.1 = f32[6,64,256]{2,1,0:T(8,128)} custom-call(f32[64,4096]{1,0:T(8,128)} %direction.1, bf16[256,4096]{1,0:T(8,128)(2,1)} %basis_ref.3, f32[5,256,256]{2,1,0:T(8,128)} %transfers_ref.3), custom_call_target="tpu_custom_call" | custom-call | flops 385875968 | bytes 5242880 | tf_op jit(solution)/shard_map/rise/pallas_call | solution.py:122
  6.4 0.5 collective-permute-start
  6.8 0.0 copy-start.3
  6.8 0.0 copy-start
  6.8 9.1 %arrange.1 = (bf16[144,4096]{1,0:T(8,128)(2,1)}, bf16[4096,128]{1,0:T(8,128)(2,1)}) custom-call(bf16[64,4096]{1,0:T(8,128)(2,1)} %points_ref.1, s32[1,4096]{1,0:T(1,128)} %bitcast.2, f32[64,4096]{1,0:T(8,128)} %direction.1), custom_call_target="tpu_custom_call" | custom-call | flops 2147483648 | bytes 5242880 | tf_op jit(solution)/shard_map/arrange/pallas_call | solution.py:79
  15.9 2.0 %collective-permute-start.7 = (bf16[144,4096]{1,0:T(8,128)(2,1)}, bf16[144,4096]{1,0:T(8,128)(2,1)S(1)}, u32[]{:S(2)}, u32[]{:S(2)}) collective-permute-start(bf16[144,4096]{1,0:T(8,128)(2,1)} %get-tuple-element.8.refs_4_), channel_id=1, source_target_pairs={{0,1},{1,2},{2,3},{3,4},{4,5},{5,6},{6,7},{7,8},{8,9},{9,10},{10,1... | collective-permute-start | bytes 3538952 | tf_op jit(solution)/shard_map/ppermute | solution.py:25
  18.0 1.3 collective-permute-start.6
  19.3 0.0 copy-done.3
  19.3 0.1 copy.14.refs_0_
  19.3 0.0 copy-start.2
  19.3 3.1 %collective-permute-start.5 = (s32[8,4]{1,0:T(8,128)S(1)}, s32[8,4]{1,0:T(8,128)S(1)}, u32[]{:S(2)}, u32[]{:S(2)}) collective-permute-start(s32[8,4]{1,0:T(8,128)S(1)} %copy.14.refs_0_), channel_id=1, source_target_pairs={{0,1},{1,2},{2,3},{3,4},{4,5},{5,6},{6,7},{7,8},{8,9},{9,10},{10,1... | collective-permute-start | bytes 392 | tf_op jit(solution)/shard_map/ppermute | solution.py:25
  22.5 0.0 collective-permute-done
  22.5 0.0 copy-done
  22.5 0.1 add.15
  22.5 1.7 %collective-permute-start.1 = (f32[5,64,256]{2,1,0:T(8,128)S(1)}, f32[5,64,256]{2,1,0:T(8,128)S(1)}, u32[]{:S(2)}, u32[]{:S(2)}) collective-permute-start(f32[5,64,256]{2,1,0:T(8,128)S(1)} %slice.36), channel_id=1, source_target_pairs={{0,2},{1,3},{2,0},{3,1},{4,6},{5,7},{6,4},{7,5},{8,10},{9,11},{10,... | collective-permute-start | bytes 983048 | tf_op jit(solution)/shard_map/ppermute | solution.py:30
  24.3 4.1 %collective-permute-done.5.refs_1_ = s32[8,4]{1,0:T(8,128)S(1)} collective-permute-done((s32[8,4]{1,0:T(8,128)S(1)}, s32[8,4]{1,0:T(8,128)S(1)}, u32[]{:S(2)}, u32[]{:S(2)}) %collective-permute-start.5) | collective-permute-done | bytes 160 | tf_op jit(solution)/shard_map/ppermute | solution.py:25
  28.4 0.0 copy-start.6
  28.4 0.0 copy-done.2
  28.4 0.6 copy-done.6
  29.0 19.9 %near_own.1.refs_7_ = f32[64,4096]{1,0:T(8,128)} custom-call(s32[8,4]{1,0:T(8,128)} %copy-done.2, s32[8,4]{1,0:T(8,128)} %copy-done.6, s32[1]{0:T(128)} %bitcast.refs_2_, bf16[4096,128]{1,0:T(8,128)(2,1)} %get-tuple-element.7.refs_3_, bf16[144,4096]{1,0:T(8,128)(2,1)} %get-tuple-element.8.refs_4_), custom_call_target="tpu_custom_call" | custom-call | flops 10737418240 | bytes 4194304 | tf_op jit(solution)/shard_map/near_own/pallas_call | solution.py:221
  48.9 6.4 %collective-permute-done.1 = f32[5,64,256]{2,1,0:T(8,128)S(1)} collective-permute-done((f32[5,64,256]{2,1,0:T(8,128)S(1)}, f32[5,64,256]{2,1,0:T(8,128)S(1)}, u32[]{:S(2)}, u32[]{:S(2)}) %collective-permute-start.1) | collective-permute-done | bytes 327712 | tf_op jit(solution)/shard_map/ppermute | solution.py:30
  55.4 13.8 %collective-permute-start.2 = (f32[4,64,256]{2,1,0:T(8,128)S(1)}, f32[4,64,256]{2,1,0:T(8,128)S(1)}, u32[]{:S(2)}, u32[]{:S(2)}) collective-permute-start(f32[4,64,256]{2,1,0:T(8,128)S(1)} %slice.38), channel_id=1, source_target_pairs={{0,4},{1,5},{2,6},{3,7},{4,0},{5,1},{6,2},{7,3},{8,12},{9,13},{10,... | collective-permute-start | bytes 786440 | tf_op jit(solution)/shard_map/ppermute | solution.py:30
  69.2 6.0 %collective-permute-done.2 = f32[4,64,256]{2,1,0:T(8,128)S(1)} collective-permute-done((f32[4,64,256]{2,1,0:T(8,128)S(1)}, f32[4,64,256]{2,1,0:T(8,128)S(1)}, u32[]{:S(2)}, u32[]{:S(2)}) %collective-permute-start.2) | collective-permute-done | bytes 262176 | tf_op jit(solution)/shard_map/ppermute | solution.py:30
  75.2 1.7 %collective-permute-start.3 = (f32[3,64,256]{2,1,0:T(8,128)S(1)}, f32[3,64,256]{2,1,0:T(8,128)S(1)}, u32[]{:S(2)}, u32[]{:S(2)}) collective-permute-start(f32[3,64,256]{2,1,0:T(8,128)S(1)} %slice.40), channel_id=1, source_target_pairs={{0,8},{1,9},{2,10},{3,11},{4,12},{5,13},{6,14},{7,15},{8,0},{9,1},... | collective-permute-start | bytes 589832 | tf_op jit(solution)/shard_map/ppermute | solution.py:30
  77.0 6.1 %collective-permute-done.3 = f32[3,64,256]{2,1,0:T(8,128)S(1)} collective-permute-done((f32[3,64,256]{2,1,0:T(8,128)S(1)}, f32[3,64,256]{2,1,0:T(8,128)S(1)}, u32[]{:S(2)}, u32[]{:S(2)}) %collective-permute-start.3) | collective-permute-done | bytes 196640 | tf_op jit(solution)/shard_map/ppermute | solution.py:30
  83.1 0.1 collective-permute-start.4
  83.2 0.0 collective-permute-done.7.refs_6_
  83.2 0.0 copy-start.4
  83.2 0.0 collective-permute-done.6.refs_5_
  83.2 1.0 copy-done.4
  84.2 0.0 copy-start.5
  84.2 1.0 copy-done.5
  85.2 12.6 %near_crossing.1.near_ref = f32[64,4096]{1,0:T(8,128)} custom-call(s32[8,4]{1,0:T(8,128)} %copy-done.2, s32[8,4]{1,0:T(8,128)} %copy-done.6, s32[1]{0:T(128)} %bitcast.refs_2_, bf16[4096,128]{1,0:T(8,128)(2,1)} %get-tuple-element.7.refs_3_, bf16[144,4096]{1,0:T(8,128)(2,1)} %get-tuple-element.8.refs_4_, bf16[144,4096]{1,0:T(8,128)(2,1)} %copy-done.5, ...), custom_call_target="tpu_custom_call" | custom-call | flops 10737418240 | bytes 4194304 | tf_op jit(solution)/shard_map/near_crossing/pallas_call | solution.py:221
  97.9 0.0 collective-permute-done.4
  97.9 0.0 copy-start.1
  97.9 0.7 copy-done.1
  98.6 28.9 %image.1 = (f32[64,4096]{1,0:T(8,128)}, f32[64,128]{1,0:T(8,128)}) custom-call(f32[6,64,256]{2,1,0:T(8,128)} %copy-done.1, f32[5,256,256]{2,1,0:T(8,128)} %transfers_ref.3, f32[6,256,256]{2,1,0:T(8,128)} %couplings_ref.1, bf16[256,4096]{1,0:T(8,128)(2,1)} %basis_ref.3, f32[64,4096]{1,0:T(8,128)} %direction.1, f32[64,4096]{1,0:T(8,128)} %residual.1, ...), custom_call_target="tpu_custom_call" | custom-call | flops 134217728 | bytes 10485760 | tf_op jit(solution)/shard_map/image/pallas_call | solution.py:334
  127.6 4.5 %update.1 = (f32[64,4096]{1,0:T(8,128)}, f32[64,4096]{1,0:T(8,128)}, f32[64,4096]{1,0:T(8,128)}) custom-call(f32[64,128]{1,0:T(8,128)} %get-tuple-element.9.factors, f32[64,4096]{1,0:T(8,128)} %solution.1, f32[64,4096]{1,0:T(8,128)} %residual.1, f32[64,4096]{1,0:T(8,128)} %direction.1, f32[64,4096]{1,0:T(8,128)} %get-tuple-element.10.image), custom_call_target="tpu_custom_call" | custom-call | tf_op jit(solution)/shard_map/update/pallas_call | solution.py:374
  (12 shorter events, 0.2 us)
Async XLA Ops:
  6.4 16.1 %collective-permute-start = (f32[6,64,256]{2,1,0:T(8,128)}, f32[6,64,256]{2,1,0:T(8,128)S(1)}, u32[]{:S(2)}, u32[]{:S(2)}) collective-permute-start(f32[6,64,256]{2,1,0:T(8,128)} %rise.1), channel_id=1, source_target_pairs={{0,1},{1,0},{2,3},{3,2},{4,5},{5,4},{6,7},{7,6},{8,9},{9,8},{10,11... | collective-permute-start | bytes 1179656 | tf_op jit(solution)/shard_map/ppermute | solution.py:30
  6.8 12.4 %copy-start.3 = (s32[8,4]{0,1:T(4,128)S(1)}, s32[8,4]{0,1:T(4,128)}, u32[]{:S(2)}) copy-start(s32[8,4]{0,1:T(4,128)} %param.11) | copy-start | bytes 388
  6.8 15.7 %copy-start = (f32[6,64,256]{2,1,0:T(8,128)S(1)}, f32[6,64,256]{2,1,0:T(8,128)}, u32[]{:S(2)}) copy-start(f32[6,64,256]{2,1,0:T(8,128)} %rise.1) | copy-start | bytes 1179652
  15.9 67.3 %collective-permute-start.7 = (bf16[144,4096]{1,0:T(8,128)(2,1)}, bf16[144,4096]{1,0:T(8,128)(2,1)S(1)}, u32[]{:S(2)}, u32[]{:S(2)}) collective-permute-start(bf16[144,4096]{1,0:T(8,128)(2,1)} %get-tuple-element.8.refs_4_), channel_id=1, source_target_pairs={{0,1},{1,2},{2,3},{3,4},{4,5},{5,6},{6,7},{7,8},{8,9},{9,10},{10,1... | collective-permute-start | bytes 3538952 | tf_op jit(solution)/shard_map/ppermute | solution.py:25
  18.0 65.2 %collective-permute-start.6 = (bf16[144,4096]{1,0:T(8,128)(2,1)}, bf16[144,4096]{1,0:T(8,128)(2,1)S(1)}, u32[]{:S(2)}, u32[]{:S(2)}) collective-permute-start(bf16[144,4096]{1,0:T(8,128)(2,1)} %get-tuple-element.8.refs_4_), channel_id=1, source_target_pairs={{1,0},{2,1},{3,2},{4,3},{5,4},{6,5},{7,6},{8,7},{9,8},{10,9},{11,1... | collective-permute-start | bytes 3538952 | tf_op jit(solution)/shard_map/ppermute | solution.py:25
  19.3 9.1 %copy-start.2 = (s32[8,4]{1,0:T(8,128)}, s32[8,4]{1,0:T(8,128)S(1)}, u32[]{:S(2)}) copy-start(s32[8,4]{1,0:T(8,128)S(1)} %copy.14.refs_0_) | copy-start | bytes 388
  19.3 9.0 %collective-permute-start.5 = (s32[8,4]{1,0:T(8,128)S(1)}, s32[8,4]{1,0:T(8,128)S(1)}, u32[]{:S(2)}, u32[]{:S(2)}) collective-permute-start(s32[8,4]{1,0:T(8,128)S(1)} %copy.14.refs_0_), channel_id=1, source_target_pairs={{0,1},{1,2},{2,3},{3,4},{4,5},{5,6},{6,7},{7,8},{8,9},{9,10},{10,1... | collective-permute-start | bytes 392 | tf_op jit(solution)/shard_map/ppermute | solution.py:25
  22.5 32.8 %collective-permute-start.1 = (f32[5,64,256]{2,1,0:T(8,128)S(1)}, f32[5,64,256]{2,1,0:T(8,128)S(1)}, u32[]{:S(2)}, u32[]{:S(2)}) collective-permute-start(f32[5,64,256]{2,1,0:T(8,128)S(1)} %slice.36), channel_id=1, source_target_pairs={{0,2},{1,3},{2,0},{3,1},{4,6},{5,7},{6,4},{7,5},{8,10},{9,11},{10,... | collective-permute-start | bytes 983048 | tf_op jit(solution)/shard_map/ppermute | solution.py:30
  28.4 0.6 copy-start.6
  55.4 19.8 %collective-permute-start.2 = (f32[4,64,256]{2,1,0:T(8,128)S(1)}, f32[4,64,256]{2,1,0:T(8,128)S(1)}, u32[]{:S(2)}, u32[]{:S(2)}) collective-permute-start(f32[4,64,256]{2,1,0:T(8,128)S(1)} %slice.38), channel_id=1, source_target_pairs={{0,4},{1,5},{2,6},{3,7},{4,0},{5,1},{6,2},{7,3},{8,12},{9,13},{10,... | collective-permute-start | bytes 786440 | tf_op jit(solution)/shard_map/ppermute | solution.py:30
  75.2 7.8 %collective-permute-start.3 = (f32[3,64,256]{2,1,0:T(8,128)S(1)}, f32[3,64,256]{2,1,0:T(8,128)S(1)}, u32[]{:S(2)}, u32[]{:S(2)}) collective-permute-start(f32[3,64,256]{2,1,0:T(8,128)S(1)} %slice.40), channel_id=1, source_target_pairs={{0,8},{1,9},{2,10},{3,11},{4,12},{5,13},{6,14},{7,15},{8,0},{9,1},... | collective-permute-start | bytes 589832 | tf_op jit(solution)/shard_map/ppermute | solution.py:30
  83.1 14.8 %collective-permute-start.4 = (f32[2,64,256]{2,1,0:T(8,128)S(1)}, f32[2,64,256]{2,1,0:T(8,128)S(1)}, u32[]{:S(2)}, u32[]{:S(2)}) collective-permute-start(f32[2,64,256]{2,1,0:T(8,128)S(1)} %slice.42), channel_id=1, source_target_pairs={{0,16},{1,17},{2,18},{3,19},{4,20},{5,21},{6,22},{7,23},{8,24},{9,... | collective-permute-start | bytes 393224 | tf_op jit(solution)/shard_map/ppermute | solution.py:30
  83.2 1.0 copy-start.4
  84.2 1.0 copy-start.5
  97.9 0.7 copy-start.1

commit v2 on v0

v2 whole, which is shorter than its diff:
```python
import functools

import jax
import jax.numpy as jnp
from jax import lax
from jax.experimental import pallas as pl
from jax.experimental.pallas import tpu as pltpu
from jax.sharding import PartitionSpec as P

SHARPNESS = 2.0
EPSILON = 1e-06
HIGHEST = lax.Precision.HIGHEST
MESH = pl.DeviceIdType.MESH
LANES = 128
EXTRA = 16
GROUP = 8
VMEM_LIMIT = 56 * 1024 * 1024
NT = (((1,), (1,)), ((), ()))


def shifted(x, axis, by):
    peers = lax.axis_size(axis)
    return lax.ppermute(x, axis, [(i, (i + by) % peers) for i in range(peers)])


def f32_dot(a, b):
    return jnp.dot(a, b, precision=HIGHEST, preferred_element_type=jnp.float32)


def f32_dot_nt(a, b):
    return lax.dot_general(a, b, NT, precision=HIGHEST, preferred_element_type=jnp.float32)


def exchange_kernel(
    count, leaf, points_ref, order_ref, direction_ref, basis_ref, transfers_hbm, couplings_hbm,
    window_ref, turned_ref, descent_ref, tall, transfers, couplings, skel, cur, arrived, coupled,
    load_sem, own_send, own_recv, stage_send, stage_recv, swap_send, swap_recv,
):
    coords, slab = points_ref.shape
    rhs = direction_ref.shape[0]
    depth = transfers.shape[0]
    bits = count.bit_length() - 1
    leaves = slab // leaf
    chunks = slab // LANES
    half = rhs // 2
    me = lax.axis_index("leaf")
    load_t = pltpu.make_async_copy(transfers_hbm, transfers, load_sem.at[0])
    load_c = pltpu.make_async_copy(couplings_hbm, couplings, load_sem.at[1])
    load_t.start()
    load_c.start()
    after, prior = (me + 1) % count, (me + count - 1) % count
    peers = [me + (1 << b) * (1 - 2 * ((me // (1 << b)) % 2)) for b in range(bits)]
    barrier = pltpu.get_barrier_semaphore()
    for peer in [after, prior] + peers:
        pl.semaphore_signal(barrier, inc=1, device_id=(peer,), device_id_type=MESH)

    value = lax.dot_general(
        direction_ref[...].astype(jnp.bfloat16),
        basis_ref[...],
        NT,
        preferred_element_type=jnp.float32,
    )
    skel[0] = value
    load_t.wait()
    for k in range(depth):
        value = f32_dot(value, transfers[k])
        skel[k + 1] = value
    pl.semaphore_wait(barrier, 2 + bits)

    mine = pl.multiple_of((me % 2) * half, half)
    other = pl.multiple_of((1 - me % 2) * half, half)

    def stage(b):
        low = min(b, depth)
        return pltpu.make_async_remote_copy(
            src_ref=skel.at[:, pl.ds(other, half)] if b == 0 else cur.at[pl.ds(low, depth + 1 - low)],
            dst_ref=arrived.at[b, pl.ds(low, depth + 1 - low)],
            send_sem=stage_send.at[b],
            recv_sem=stage_recv.at[b],
            device_id=(peers[b],),
            device_id_type=MESH,
        )

    def place(j, slot):
        return pl.ds(pl.multiple_of(slot * slab + j * leaf, leaf), leaf)

    def to_prior(j):
        return pltpu.make_async_remote_copy(
            src_ref=window_ref.at[:, place(j, 1)],
            dst_ref=window_ref.at[:, place(j, 2)],
            send_sem=own_send.at[0, j],
            recv_sem=own_recv.at[0, j],
            device_id=(prior,),
            device_id_type=MESH,
        )

    def to_after(j):
        return pltpu.make_async_remote_copy(
            src_ref=window_ref.at[:, place(j, 1)],
            dst_ref=window_ref.at[:, place(j, 0)],
            send_sem=own_send.at[1, j],
            recv_sem=own_recv.at[1, j],
            device_id=(after,),
            device_id_type=MESH,
        )

    def arrange(j, carry):
        cols = pl.ds(pl.multiple_of(j * leaf, leaf), leaf)
        order = order_ref[:, cols]
        high = order // LANES
        low = order - high * LANES
        rows = lax.broadcasted_iota(jnp.int32, (LANES, leaf), 0)
        onehot = jnp.where(rows == low, 1.0, 0.0).astype(jnp.bfloat16)
        picked = jnp.zeros((coords, leaf), jnp.float32)
        step = 4
        for c in range(0, chunks, step):
            part = jnp.dot(
                tall[c * coords : (c + step) * coords, :], onehot, preferred_element_type=jnp.float32
            )
            for h in range(step):
                picked = jnp.where(high == c + h, part[h * coords : (h + 1) * coords], picked)
        square = -0.5 * jnp.sum(picked * picked, axis=0, keepdims=True)
        first = square.astype(jnp.bfloat16).astype(jnp.float32)
        second = (square - first).astype(jnp.bfloat16).astype(jnp.float32)
        third = (square - first - second).astype(jnp.bfloat16).astype(jnp.float32)

        def extra(height, at_parts, at_ones):
            row = lax.broadcasted_iota(jnp.int32, (height, leaf), 0)
            out = jnp.where((row >= at_ones) & (row < at_ones + 3), 1.0, 0.0)
            for i, piece in enumerate((first, second, third)):
                out = jnp.where(row == at_parts + i, piece, out)
            return out

        here = place(j, 1)
        window_ref[0:coords, here] = picked.astype(jnp.bfloat16)
        window_ref[coords : coords + EXTRA, here] = extra(EXTRA, 0, 3).astype(jnp.bfloat16)
        window_ref[coords + EXTRA :, here] = direction_ref[:, cols].astype(jnp.bfloat16)

        @pl.when(me > 0)
        def _():
            to_prior(j).start()

        @pl.when(me < count - 1)
        def _():
            to_after(j).start()

        wide = jnp.concatenate([picked, extra(LANES - coords, 3, 0)], axis=0)
        turned_ref[cols, :] = (2.0 * SHARPNESS * wide.T).astype(jnp.bfloat16)
        return carry

    def swap(k):
        return pltpu.make_async_remote_copy(
            src_ref=coupled.at[k, me % 2],
            dst_ref=coupled.at[k, me % 2],
            send_sem=swap_send.at[k],
            recv_sem=swap_recv.at[k],
            device_id=(peers[0],),
            device_id_type=MESH,
        )

    def couple(k):
        coupled[k, me % 2] = f32_dot_nt(f32_dot(cur[k], couplings[k]), couplings[k])
        swap(k).start()

    def both_halves(k):
        swap(k).wait()
        return coupled[k].reshape(rhs, coupled.shape[-1])

    stage(0).start()
    for h in range(chunks):
        tall[h * coords : (h + 1) * coords, :] = points_ref[:, h * LANES : (h + 1) * LANES]
    done = 0
    for b in range(bits):
        upto = min(leaves, -(-leaves * (b + 1) // min(bits, depth)))
        if upto > done:
            lax.fori_loop(done, upto, arrange, 0)
        done = upto
        stage(b).wait()
        low = min(b, depth)
        if b == 0:
            cur[...] = skel[:, pl.ds(mine, half)] + arrived[0]
        else:
            cur[low:] = cur[low:] + arrived[b, low:]
        if b + 1 < bits:
            stage(b + 1).start()
        if b == 0:
            load_c.wait()
        if b < depth:
            couple(b)
    couple(depth)
    descent = both_halves(depth)
    for k in reversed(range(depth)):
        descent = f32_dot_nt(descent, transfers[k]) + both_halves(k)
    descent_ref[...] = descent.astype(jnp.bfloat16)

    def finish(j, carry):
        @pl.when(me > 0)
        def _():
            to_prior(j).wait_send()
            to_after(j).wait_recv()

        @pl.when(me < count - 1)
        def _():
            to_after(j).wait_send()
            to_prior(j).wait_recv()

        return carry

    lax.fori_loop(0, leaves, finish, 0)


def exchange(points, leaf_order, direction, basis, transfers, couplings, leaf):
    count = lax.axis_size("leaf")
    bits = count.bit_length() - 1
    coords, slab = points.shape
    rhs = direction.shape[0]
    depth, rank = transfers.shape[:2]
    leaves = slab // leaf
    height = coords + EXTRA + rhs
    vmem = pl.BlockSpec(memory_space=pltpu.VMEM)
    hbm = pl.BlockSpec(memory_space=pl.ANY)
    half = (depth + 1, rhs // 2, rank)
    return pl.pallas_call(
        functools.partial(exchange_kernel, count, leaf),
        in_specs=[vmem] * 4 + [hbm] * 2,
        out_specs=[vmem] * 3,
        out_shape=[
            jax.ShapeDtypeStruct((height, 3 * slab), jnp.bfloat16),
            jax.ShapeDtypeStruct((slab, LANES), jnp.bfloat16),
            jax.ShapeDtypeStruct((rhs, rank), jnp.bfloat16),
        ],
        scratch_shapes=[
            pltpu.VMEM((slab // LANES * coords, LANES), jnp.bfloat16),
            pltpu.VMEM(transfers.shape, jnp.float32),
            pltpu.VMEM(couplings.shape, jnp.float32),
            pltpu.VMEM((depth + 1, rhs, rank), jnp.float32),
            pltpu.VMEM(half, jnp.float32),
            pltpu.VMEM((bits,) + half, jnp.float32),
            pltpu.VMEM((depth + 1, 2, rhs // 2, rank), jnp.float32),
            pltpu.SemaphoreType.DMA((2,)),
            pltpu.SemaphoreType.DMA((2, leaves)),
            pltpu.SemaphoreType.DMA((2, leaves)),
            pltpu.SemaphoreType.DMA((bits,)),
            pltpu.SemaphoreType.DMA((bits,)),
            pltpu.SemaphoreType.DMA((depth + 1,)),
            pltpu.SemaphoreType.DMA((depth + 1,)),
        ],
        compiler_params=pltpu.CompilerParams(
            vmem_limit_bytes=VMEM_LIMIT, collective_id=1, has_side_effects=True
        ),
        cost_estimate=pl.CostEstimate(
            flops=2 * coords * slab * slab, bytes_accessed=10 << 20, transcendentals=0
        ),
        name="exchange",
    )(points, leaf_order.reshape(1, slab), direction, basis, transfers, couplings)


def near_kernel(
    coords, lists, before, first_ref, turned, window, descent, basis, direction, residual,
    image_ref, sums_ref, acc, slots,
):
    leaves, partners = lists.shape
    leaf = turned.shape[0]
    rhs = direction.shape[0]
    deep = coords + EXTRA
    target = pl.program_id(0)
    whole_id = first_ref[0] + target

    def lists_me(ref, row):
        found = ref[row, 0] == whole_id
        for m in range(1, partners):
            found = found | (ref[row, m] == whole_id)
        return found

    known = jnp.int32(0)
    for m in range(partners):
        slots[known] = lists[target, m] - first_ref[0] + leaves
        known += jnp.where(lists[target, m] >= 0, 1, 0)
    for ref, at in ((lists, leaves), (before, 0)):
        for a in range(leaves):
            slots[known] = a + at
            known += jnp.where(lists_me(ref, a), 1, 0)
    slots[known] = target + leaves
    slots[known + 1] = target + leaves
    acc[...] = jnp.zeros_like(acc)
    rows = 128

    def two(i, carry):
        cols, weights = [], []
        for s in range(2):
            at = 2 * i + s
            cols.append(pl.ds(pl.multiple_of(slots[at] * leaf, leaf), leaf))
            weight = jnp.where(at < known, 1, jnp.where(at == known, 1 + known, 0))
            weights.append(weight.astype(jnp.float32))
        for r in range(0, leaf, rows):
            total = acc[r : r + rows, :]
            for col, weight in zip(cols, weights):
                exponent = jnp.dot(
                    turned[r : r + rows, 0:deep],
                    window[0:deep, col],
                    preferred_element_type=jnp.float32,
                )
                tile = jnp.exp(exponent).astype(jnp.bfloat16)
                total += weight * lax.dot_general(
                    tile, window[deep:, col], NT, preferred_element_type=jnp.float32
                )
            acc[r : r + rows, :] = total
        return carry

    lax.fori_loop(0, (known + 2) // 2, two, 0)
    d = direction[...]
    r = residual[...]
    image = d + acc[...].T + jnp.dot(descent[...], basis[...], preferred_element_type=jnp.float32)
    image_ref[...] = image

    @pl.when(target == 0)
    def _():
        sums_ref[...] = jnp.zeros_like(sums_ref)

    for q, (x, y) in enumerate(((r, r), (d, image), (r, image), (image, image))):
        both = x * y
        sums_ref[q] += sum(both[:, i : i + LANES] for i in range(0, leaf, LANES))


def near_and_image(lists, before, first, turned, window, descent, basis, direction, residual, coords):
    leaves, partners = lists.shape
    rhs, slab = direction.shape
    rank = basis.shape[0]
    leaf = slab // leaves
    smem = pl.BlockSpec(memory_space=pltpu.SMEM)
    vmem = pl.BlockSpec(memory_space=pltpu.VMEM)
    block = pl.BlockSpec((rhs, leaf), lambda j: (0, j))
    return pl.pallas_call(
        functools.partial(near_kernel, coords),
        grid=(leaves,),
        in_specs=[
            smem, smem, smem,
            pl.BlockSpec((leaf, LANES), lambda j: (j, 0)),
            vmem, vmem,
            pl.BlockSpec((rank, leaf), lambda j: (0, j)),
            block, block,
        ],
        out_specs=[block, pl.BlockSpec((4, rhs, LANES), lambda j: (0, 0, 0))],
        out_shape=[
            jax.ShapeDtypeStruct((rhs, slab), jnp.float32),
            jax.ShapeDtypeStruct((4, rhs, LANES), jnp.float32),
        ],
        scratch_shapes=[
            pltpu.VMEM((leaf, rhs), jnp.float32),
            pltpu.SMEM((partners + 2 * leaves + 2,), jnp.int32),
        ],
        compiler_params=pltpu.CompilerParams(vmem_limit_bytes=VMEM_LIMIT),
        name="near",
    )(lists, before, first, turned, window, descent, basis, direction, residual)


def reduce_kernel(
    count, sums_ref, factors_ref, tall, inner, outer, send_in, recv_in, send_out, recv_out
):
    me = lax.axis_index("leaf")
    groups = count // GROUP
    base = (me // GROUP) * GROUP
    in_peers = [base + (me - base + d) % GROUP for d in range(1, GROUP)]
    out_peers = [(me + GROUP * e) % count for e in range(1, groups)]
    barrier = pltpu.get_barrier_semaphore()
    for peer in in_peers + out_peers:
        pl.semaphore_signal(barrier, inc=1, device_id=(peer,), device_id_type=MESH)

    rhs = sums_ref.shape[1]
    sums = [sums_ref[q] for q in range(4)]
    zero = jnp.zeros((rhs, LANES), jnp.float32)
    lane = lax.broadcasted_iota(jnp.int32, (rhs, LANES), 1)
    packed = zero
    for i, s in enumerate(sums):
        packed = jnp.where(lane == i, jnp.sum(s, axis=1, keepdims=True), packed)
    tall[...] = jnp.zeros_like(tall)
    tall[0:rhs, :] = packed
    inner[0] = tall[...].T[0:8, :]

    pl.semaphore_wait(barrier, len(in_peers) + len(out_peers))

    def all_sum(buffer, peers, send, recv):
        copies = []
        for i, peer in enumerate(peers):
            copy = pltpu.make_async_remote_copy(
                src_ref=buffer.at[0],
                dst_ref=buffer.at[i + 1],
                send_sem=send.at[i],
                recv_sem=recv.at[i],
                device_id=(peer,),
                device_id_type=MESH,
            )
            copy.start()
            copies.append(copy)
        for copy in copies:
            copy.wait()
        total = buffer[0]
        for i in range(len(peers)):
            total = total + buffer[i + 1]
        return total

    total = all_sum(inner, in_peers, send_in, recv_in)
    if groups > 1:
        outer[0] = total
        total = all_sum(outer, out_peers, send_out, recv_out)
    old = total[0:1]
    step = old / (total[1:2] + EPSILON)
    new = jnp.maximum(old - 2.0 * step * total[2:3] + step * step * total[3:4], 0.0)
    ratio = new / (old + EPSILON)
    row = lax.broadcasted_iota(jnp.int32, (LANES, LANES), 0)
    both = jnp.where(row == 0, step, jnp.where(row == 1, ratio, 0.0))
    factors_ref[...] = both.T[0:rhs, :]


def reduce(sums):
    count = lax.axis_size("leaf")
    groups = count // GROUP
    rhs = sums.shape[1]
    vmem = pl.BlockSpec(memory_space=pltpu.VMEM)
    return pl.pallas_call(
        functools.partial(reduce_kernel, count),
        in_specs=[vmem],
        out_specs=vmem,
        out_shape=jax.ShapeDtypeStruct((rhs, LANES), jnp.float32),
        scratch_shapes=[
            pltpu.VMEM((LANES, LANES), jnp.float32),
            pltpu.VMEM((GROUP, 8, LANES), jnp.float32),
            pltpu.VMEM((max(groups, 2), 8, LANES), jnp.float32),
            pltpu.SemaphoreType.DMA((GROUP - 1,)),
            pltpu.SemaphoreType.DMA((GROUP - 1,)),
            pltpu.SemaphoreType.DMA((max(groups - 1, 1),)),
            pltpu.SemaphoreType.DMA((max(groups - 1, 1),)),
        ],
        compiler_params=pltpu.CompilerParams(
            vmem_limit_bytes=VMEM_LIMIT, collective_id=0, has_side_effects=True
        ),
        name="reduce",
    )(sums)


def update_kernel(factors, solution, residual, direction, image, new_solution, new_residual, new_direction):
    step = factors[:, 0:1]
    ratio = factors[:, 1:2]
    d = direction[...]
    new_solution[...] = solution[...] + step * d
    r = residual[...] - step * image[...]
    new_residual[...] = r
    new_direction[...] = r + ratio * d


def update(factors, solution, residual, direction, image):
    rhs, slab = direction.shape
    width = slab // 4
    block = pl.BlockSpec((rhs, width), lambda j: (0, j))
    shape = jax.ShapeDtypeStruct((rhs, slab), jnp.float32)
    return pl.pallas_call(
        update_kernel,
        grid=(slab // width,),
        in_specs=[pl.BlockSpec((rhs, LANES), lambda j: (0, 0))] + [block] * 4,
        out_specs=[block] * 3,
        out_shape=[shape] * 3,
        compiler_params=pltpu.CompilerParams(vmem_limit_bytes=VMEM_LIMIT),
        name="update",
    )(factors, solution, residual, direction, image)


def local(
    points, leaf_order, near_pairs, solution, residual, direction, skeleton_basis, transfers, couplings
):
    leaves = near_pairs.shape[0]
    leaf = points.shape[1] // leaves
    first = (lax.axis_index("leaf") * leaves).astype(jnp.int32).reshape(1)
    before = shifted(near_pairs, "leaf", 1)
    window, turned, descent = exchange(
        points, leaf_order, direction, skeleton_basis, transfers, couplings, leaf
    )
    image, sums = near_and_image(
        near_pairs, before, first, turned, window, descent, skeleton_basis, direction, residual,
        points.shape[0],
    )
    factors = reduce(sums)
    return tuple(update(factors, solution, residual, direction, image))


def solution(mesh):
    in_specs = (
        P(None, "leaf"),
        P("leaf"),
        P("leaf", None),
        P(None, "leaf"),
        P(None, "leaf"),
        P(None, "leaf"),
        P(None, "leaf"),
        P("leaf", None, None),
        P(),
    )
    out_specs = (P(None, "leaf"), P(None, "leaf"), P(None, "leaf"))
    return jax.shard_map(local, mesh=mesh, in_specs=in_specs, out_specs=out_specs, check_vma=False)
```

time: 534 us -> 105 us (0.20)
  local copies, waits for them, and re-layouts: 203 us -> 1.35 us
  waiting for transfers between devices: 116 us -> 0.01 us
  Pallas kernels: 0 us -> 101 us
  blocking collectives: 84.1 us -> 0 us
  matrix products: 62.8 us -> 0 us
  other arithmetic: 18.4 us -> 0 us
  loops' own time: 17.3 us -> 0 us
  between operations: 14.5 us -> 0.68 us
  starting transfers between devices: 11.8 us -> 0.45 us
    dynamic_update_slice x32 -> x0, local copies, waits for them, and re-layouts: 133 us -> none  [leaf_terms(): return lax.map(per_leaf, (sources, others, src_weight, other_weight))]
    pallas_call x0 -> x4, Pallas kernels: none -> 101 us  [the longest x1 46.2 us: exchange(): pl.pallas_call(functools.partial(exchange_kernel, count, leaf), in_specs=...]
    psum x1 -> x0, waiting for transfers between devices: 95.9 us -> none  [local(): top_total, old_norm = lax.psum((skeletons[tree_depth], local_norm), 'leaf')]
    psum x2 -> x0, blocking collectives: 84.1 us -> none  [the longest x1 43.4 us: local(): top_total, old_norm = lax.psum((skeletons[tree_depth], local_norm), 'leaf')]
    dot_general x50 -> x0, matrix products: 62.8 us -> none  [the longest x8 21 us: per_leaf(): jnp.einsum('dk,dnj->nkj', source_pts, partner_pts, preferred_element_type...]
    gather x25 -> x0, local copies, waits for them, and re-layouts: 48.2 us -> none  [the longest x1 15 us: local(): tree_points = jnp.take(points, leaf_order, axis=1)]
    ppermute x8 -> x1, waiting for transfers between devices: 20.3 us -> 0.01 us  [shifted(): return lax.ppermute(x, axis, [(i, (i + by) % peers) for i in range(peers)])]
    another operation x1 -> x0, loops' own time: 17.3 us -> none  [leaf_terms(): return lax.map(per_leaf, (sources, others, src_weight, other_weight))]
  transfers between devices with their start and end apart: 9 -> 1, of which waited for: 5 -> 0; matrix products, arithmetic and copies ran while one was open for 8% -> 0% of each run, Pallas kernels for 0% -> 45%
where the time goes in v2:
time: 105 us; the launch traced here: 104 us
  Pallas kernels  101 us (96%)
  local copies, waits for them, and re-layouts  1.35 us (1%)
    pallas_call x1, Pallas kernels, exchange(): pl.pallas_call(functools.partial(exchange_kernel, count, leaf), in_specs=...  46.2 us
    pallas_call x1, Pallas kernels, near_and_image(): pl.pallas_call(functools.partial(near_kernel, coords), grid=(leaves,), in...  34.6 us
    pallas_call x1, Pallas kernels, reduce(): pl.pallas_call(functools.partial(reduce_kernel, count), in_specs=[vmem],...  15.9 us
    pallas_call x1, Pallas kernels, update(): pl.pallas_call(update_kernel, grid=(slab // width,), in_specs=[pl.BlockSp...  4.49 us
  transfers between devices with their start and end apart: 1, of which 0 were waited for; matrix products, arithmetic and copies ran while one was open for 0% of the time, Pallas kernels for 45%

profile of v2, /device:TPU:0, one launch (start us, length us, event | category | flops | bytes accessed | tf_op | source)
XLA Modules:
  0.0 103.6 jit_solution(1667103790251185267)
XLA Ops:
  0.6 0.8 copy.13.lists
  1.4 0.0 copy-start
  1.4 0.5 collective-permute-start
  1.8 46.2 %exchange.1 = (bf16[144,12288]{1,0:T(8,128)(2,1)}, bf16[4096,128]{1,0:T(8,128)(2,1)}, bf16[64,256]{1,0:T(8,128)(2,1)}) custom-call(bf16[64,4096]{1,0:T(8,128)(2,1)} %points_ref.1, s32[1,4096]{1,0:T(1,128)} %bitcast.2, f32[64,4096]{1,0:T(8,128)} %direction.3, bf16[256,4096]{1,0:T(8,128)(2,1)} %basis.1, f32[5,256,256]{2,1,0:T(8,128)} %transfers_hbm.1, ...), custom_call_target="tpu_custom_call" | custom-call | flops 2147483648 | bytes 10485760 | tf_op jit(solution)/shard_map/exchange/pallas_call | solution.py:223
  48.1 0.0 copy-done
  48.1 0.0 collective-permute-done.before
  48.1 0.0 copy-start.1
  48.1 0.6 copy-done.1
  48.7 34.6 %near.1 = (f32[64,4096]{1,0:T(8,128)}, f32[4,64,128]{2,1,0:T(8,128)}) custom-call(s32[8,4]{1,0:T(8,128)} %copy-done, s32[8,4]{1,0:T(8,128)} %copy-done.1, s32[1]{0:T(128)} %bitcast.first_ref, bf16[4096,128]{1,0:T(8,128)(2,1)} %get-tuple-element.8.turned, bf16[144,12288]{1,0:T(8,128)(2,1)} %get-tuple-element.9.window, ...), custom_call_target="tpu_custom_call" | custom-call | tf_op jit(solution)/shard_map/near/pallas_call | solution.py:333
  83.2 15.9 %reduce.1.factors = f32[64,128]{1,0:T(8,128)} custom-call(f32[4,64,128]{2,1,0:T(8,128)} %get-tuple-element.11.sums_ref), custom_call_target="tpu_custom_call" | custom-call | tf_op jit(solution)/shard_map/reduce/pallas_call | solution.py:420
  99.1 4.5 %update.1 = (f32[64,4096]{1,0:T(8,128)}, f32[64,4096]{1,0:T(8,128)}, f32[64,4096]{1,0:T(8,128)}) custom-call(f32[64,128]{1,0:T(8,128)} %reduce.1.factors, f32[64,4096]{1,0:T(8,128)} %solution.1, f32[64,4096]{1,0:T(8,128)} %residual.3, f32[64,4096]{1,0:T(8,128)} %direction.3, f32[64,4096]{1,0:T(8,128)} %get-tuple-element.12.image), custom_call_target="tpu_custom_call" | custom-call | tf_op jit(solution)/shard_map/update/pallas_call | solution.py:456
Async XLA Ops:
  1.4 46.7 %copy-start = (s32[8,4]{1,0:T(8,128)}, s32[8,4]{1,0:T(8,128)S(1)}, u32[]{:S(2)}) copy-start(s32[8,4]{1,0:T(8,128)S(1)} %copy.13.lists) | copy-start | bytes 388
  1.4 46.7 %collective-permute-start = (s32[8,4]{1,0:T(8,128)S(1)}, s32[8,4]{1,0:T(8,128)S(1)}, u32[]{:S(2)}, u32[]{:S(2)}) collective-permute-start(s32[8,4]{1,0:T(8,128)S(1)} %copy.13.lists), channel_id=1, source_target_pairs={{0,1},{1,2},{2,3},{3,4},{4,5},{5,6},{6,7},{7,8},{8,9},{9,10},{10,1... | collective-permute-start | bytes 392 | tf_op jit(solution)/shard_map/ppermute | solution.py:23
  48.1 0.6 copy-start.1

commit v3 on v2

--- a/solution.py
+++ b/solution.py
@@ -54,17 +54,8 @@
     for peer in [after, prior] + peers:
         pl.semaphore_signal(barrier, inc=1, device_id=(peer,), device_id_type=MESH)
 
-    value = lax.dot_general(
-        direction_ref[...].astype(jnp.bfloat16),
-        basis_ref[...],
-        NT,
-        preferred_element_type=jnp.float32,
-    )
-    skel[0] = value
-    load_t.wait()
-    for k in range(depth):
-        value = f32_dot(value, transfers[k])
-        skel[k + 1] = value
+    for h in range(chunks):
+        tall[h * coords : (h + 1) * coords, :] = points_ref[:, h * LANES : (h + 1) * LANES]
     pl.semaphore_wait(barrier, 2 + bits)
 
     mine = pl.multiple_of((me % 2) * half, half)
@@ -166,12 +157,22 @@
         swap(k).wait()
         return coupled[k].reshape(rhs, coupled.shape[-1])
 
+    done = (leaves + 1) // 2
+    lax.fori_loop(0, done, arrange, 0)
+    value = lax.dot_general(
+        direction_ref[...].astype(jnp.bfloat16),
+        basis_ref[...],
+        NT,
+        preferred_element_type=jnp.float32,
+    )
+    skel[0] = value
+    load_t.wait()
+    for k in range(depth):
+        value = f32_dot(value, transfers[k])
+        skel[k + 1] = value
     stage(0).start()
-    for h in range(chunks):
-        tall[h * coords : (h + 1) * coords, :] = points_ref[:, h * LANES : (h + 1) * LANES]
-    done = 0
     for b in range(bits):
-        upto = min(leaves, -(-leaves * (b + 1) // min(bits, depth)))
+        upto = leaves if b + 1 == min(bits, depth) else min(leaves, done + 1)
         if upto > done:
             lax.fori_loop(done, upto, arrange, 0)
         done = upto
@@ -283,7 +284,7 @@
     slots[known] = target + leaves
     slots[known + 1] = target + leaves
     acc[...] = jnp.zeros_like(acc)
-    rows = 128
+    rows = leaf
 
     def two(i, carry):
         cols, weights = [], []
@@ -450,7 +451,7 @@
 
 def update(factors, solution, residual, direction, image):
     rhs, slab = direction.shape
-    width = slab // 4
+    width = slab // 8
     block = pl.BlockSpec((rhs, width), lambda j: (0, j))
     shape = jax.ShapeDtypeStruct((rhs, slab), jnp.float32)
     return pl.pallas_call(

time: 105 us -> 110 us (1.048)
  Pallas kernels: 101 us -> 107 us
    pallas_call x1, Pallas kernels: 46.2 us -> 52.5 us  [exchange(): pl.pallas_call(functools.partial(exchange_kernel, count, leaf), in_specs=...]
    pallas_call x1, Pallas kernels: 34.6 us -> 29.7 us  [near_and_image(): pl.pallas_call(functools.partial(near_kernel, coords), grid=(leaves,), in...]
    pallas_call x1, Pallas kernels: 15.9 us -> 18.3 us  [reduce(): pl.pallas_call(functools.partial(reduce_kernel, count), in_specs=[vmem],...]
    pallas_call x1, Pallas kernels: 4.49 us -> 6.64 us  [update(): pl.pallas_call(update_kernel, grid=(slab // width,), in_specs=[pl.BlockSp...]
  transfers between devices with their start and end apart: 1 -> 1, of which waited for: 0 -> 0; matrix products, arithmetic and copies ran while one was open for 0% -> 0% of each run, Pallas kernels for 45% -> 48%
where the time goes in v3:
time: 110 us
  Pallas kernels  107 us (97%)
  local copies, waits for them, and re-layouts  1.35 us (1%)
    pallas_call x1, Pallas kernels, exchange(): pl.pallas_call(functools.partial(exchange_kernel, count, leaf), in_specs=...  52.5 us
    pallas_call x1, Pallas kernels, near_and_image(): pl.pallas_call(functools.partial(near_kernel, coords), grid=(leaves,), in...  29.7 us
    pallas_call x1, Pallas kernels, reduce(): pl.pallas_call(functools.partial(reduce_kernel, count), in_specs=[vmem],...  18.3 us
    pallas_call x1, Pallas kernels, update(): pl.pallas_call(update_kernel, grid=(slab // width,), in_specs=[pl.BlockSp...  6.64 us
  transfers between devices with their start and end apart: 1, of which 0 were waited for; matrix products, arithmetic and copies ran while one was open for 0% of the time, Pallas kernels for 48%

profile of v3, /device:TPU:0, one launch (start us, length us, event | category | flops | bytes accessed | tf_op | source)
XLA Modules:
  0.0 109.5 jit_solution(8108768873437278603)
XLA Ops:
  0.6 0.8 copy.13.lists
  1.4 0.0 copy-start
  1.4 0.5 collective-permute-start
  1.8 52.5 %exchange.1 = (bf16[144,12288]{1,0:T(8,128)(2,1)}, bf16[4096,128]{1,0:T(8,128)(2,1)}, bf16[64,256]{1,0:T(8,128)(2,1)}) custom-call(bf16[64,4096]{1,0:T(8,128)(2,1)} %points_ref.1, s32[1,4096]{1,0:T(1,128)} %bitcast.2, f32[64,4096]{1,0:T(8,128)} %direction.3, bf16[256,4096]{1,0:T(8,128)(2,1)} %basis.1, f32[5,256,256]{2,1,0:T(8,128)} %transfers_hbm.1, ...), custom_call_target="tpu_custom_call" | custom-call | flops 2147483648 | bytes 10485760 | tf_op jit(solution)/shard_map/exchange/pallas_call | solution.py:224
  54.3 0.0 copy-done
  54.3 0.0 collective-permute-done.before
  54.3 0.0 copy-start.1
  54.3 0.6 copy-done.1
  54.9 29.7 %near.1 = (f32[64,4096]{1,0:T(8,128)}, f32[4,64,128]{2,1,0:T(8,128)}) custom-call(s32[8,4]{1,0:T(8,128)} %copy-done, s32[8,4]{1,0:T(8,128)} %copy-done.1, s32[1]{0:T(128)} %bitcast.first_ref, bf16[4096,128]{1,0:T(8,128)(2,1)} %get-tuple-element.8.turned, bf16[144,12288]{1,0:T(8,128)(2,1)} %get-tuple-element.9.window, ...), custom_call_target="tpu_custom_call" | custom-call | tf_op jit(solution)/shard_map/near/pallas_call | solution.py:334
  84.6 18.3 %reduce.1.factors = f32[64,128]{1,0:T(8,128)} custom-call(f32[4,64,128]{2,1,0:T(8,128)} %get-tuple-element.11.sums_ref), custom_call_target="tpu_custom_call" | custom-call | tf_op jit(solution)/shard_map/reduce/pallas_call | solution.py:421
  102.9 6.6 %update.1 = (f32[64,4096]{1,0:T(8,128)}, f32[64,4096]{1,0:T(8,128)}, f32[64,4096]{1,0:T(8,128)}) custom-call(f32[64,128]{1,0:T(8,128)} %reduce.1.factors, f32[64,4096]{1,0:T(8,128)} %solution.1, f32[64,4096]{1,0:T(8,128)} %residual.3, f32[64,4096]{1,0:T(8,128)} %direction.3, f32[64,4096]{1,0:T(8,128)} %get-tuple-element.12.image), custom_call_target="tpu_custom_call" | custom-call | tf_op jit(solution)/shard_map/update/pallas_call | solution.py:457
Async XLA Ops:
  1.4 52.9 %copy-start = (s32[8,4]{1,0:T(8,128)}, s32[8,4]{1,0:T(8,128)S(1)}, u32[]{:S(2)}) copy-start(s32[8,4]{1,0:T(8,128)S(1)} %copy.13.lists) | copy-start | bytes 388
  1.4 52.9 %collective-permute-start = (s32[8,4]{1,0:T(8,128)S(1)}, s32[8,4]{1,0:T(8,128)S(1)}, u32[]{:S(2)}, u32[]{:S(2)}) collective-permute-start(s32[8,4]{1,0:T(8,128)S(1)} %copy.13.lists), channel_id=1, source_target_pairs={{0,1},{1,2},{2,3},{3,4},{4,5},{5,6},{6,7},{7,8},{8,9},{9,10},{10,1... | collective-permute-start | bytes 392 | tf_op jit(solution)/shard_map/ppermute | solution.py:23
  54.3 0.6 copy-start.1

commit v4 on v2

--- a/solution.py
+++ b/solution.py
@@ -136,6 +136,11 @@
         window_ref[coords : coords + EXTRA, here] = extra(EXTRA, 0, 3).astype(jnp.bfloat16)
         window_ref[coords + EXTRA :, here] = direction_ref[:, cols].astype(jnp.bfloat16)
 
+        wide = jnp.concatenate([picked, extra(LANES - coords, 3, 0)], axis=0)
+        turned_ref[cols, :] = (2.0 * SHARPNESS * wide.T).astype(jnp.bfloat16)
+        return carry
+
+    def send(j, carry):
         @pl.when(me > 0)
         def _():
             to_prior(j).start()
@@ -144,8 +149,6 @@
         def _():
             to_after(j).start()
 
-        wide = jnp.concatenate([picked, extra(LANES - coords, 3, 0)], axis=0)
-        turned_ref[cols, :] = (2.0 * SHARPNESS * wide.T).astype(jnp.bfloat16)
         return carry
 
     def swap(k):
@@ -171,7 +174,7 @@
         tall[h * coords : (h + 1) * coords, :] = points_ref[:, h * LANES : (h + 1) * LANES]
     done = 0
     for b in range(bits):
-        upto = min(leaves, -(-leaves * (b + 1) // min(bits, depth)))
+        upto = min(leaves, -(-leaves * (b + 1) // 2))
         if upto > done:
             lax.fori_loop(done, upto, arrange, 0)
         done = upto
@@ -183,6 +186,8 @@
             cur[low:] = cur[low:] + arrived[b, low:]
         if b + 1 < bits:
             stage(b + 1).start()
+        if b == 1:
+            lax.fori_loop(0, leaves, send, 0)
         if b == 0:
             load_c.wait()
         if b < depth:
@@ -283,7 +288,7 @@
     slots[known] = target + leaves
     slots[known + 1] = target + leaves
     acc[...] = jnp.zeros_like(acc)
-    rows = 128
+    rows = leaf
 
     def two(i, carry):
         cols, weights = [], []
@@ -450,13 +455,13 @@
 
 def update(factors, solution, residual, direction, image):
     rhs, slab = direction.shape
-    width = slab // 4
-    block = pl.BlockSpec((rhs, width), lambda j: (0, j))
+    height = rhs // 4
+    block = pl.BlockSpec((height, slab), lambda j: (j, 0))
     shape = jax.ShapeDtypeStruct((rhs, slab), jnp.float32)
     return pl.pallas_call(
         update_kernel,
-        grid=(slab // width,),
-        in_specs=[pl.BlockSpec((rhs, LANES), lambda j: (0, 0))] + [block] * 4,
+        grid=(rhs // height,),
+        in_specs=[pl.BlockSpec((height, LANES), lambda j: (j, 0))] + [block] * 4,
         out_specs=[block] * 3,
         out_shape=[shape] * 3,
         compiler_params=pltpu.CompilerParams(vmem_limit_bytes=VMEM_LIMIT),

time: 105 us -> 106 us (level); the launches traced: 104 us -> 106 us
  Pallas kernels: 101 us -> 103 us
    pallas_call x1, Pallas kernels: 46.2 us -> 50.5 us  [exchange(): pl.pallas_call(functools.partial(exchange_kernel, count, leaf), in_specs=...]
    pallas_call x1, Pallas kernels: 34.6 us -> 31.3 us  [near_and_image(): pl.pallas_call(functools.partial(near_kernel, coords), grid=(leaves,), in...]
    pallas_call x1, Pallas kernels: 15.9 us -> 17.2 us  [reduce(): pl.pallas_call(functools.partial(reduce_kernel, count), in_specs=[vmem],...]
  transfers between devices with their start and end apart: 1 -> 1, of which waited for: 0 -> 0; matrix products, arithmetic and copies ran while one was open for 0% -> 0% of each run, Pallas kernels for 45% -> 48%
where the time goes in v4:
time: 106 us
  Pallas kernels  103 us (97%)
  local copies, waits for them, and re-layouts  1.35 us (1%)
    pallas_call x1, Pallas kernels, exchange(): pl.pallas_call(functools.partial(exchange_kernel, count, leaf), in_specs=...  50.5 us
    pallas_call x1, Pallas kernels, near_and_image(): pl.pallas_call(functools.partial(near_kernel, coords), grid=(leaves,), in...  31.3 us
    pallas_call x1, Pallas kernels, reduce(): pl.pallas_call(functools.partial(reduce_kernel, count), in_specs=[vmem],...  17.2 us
    pallas_call x1, Pallas kernels, update(): pl.pallas_call(update_kernel, grid=(rhs // height,), in_specs=[pl.BlockSp...  4.54 us
  transfers between devices with their start and end apart: 1, of which 0 were waited for; matrix products, arithmetic and copies ran while one was open for 0% of the time, Pallas kernels for 48%

profile of v4, /device:TPU:0, one launch (start us, length us, event | category | flops | bytes accessed | tf_op | source)
XLA Modules:
  0.0 105.9 jit_solution(757186299055948872)
XLA Ops:
  0.6 0.8 copy.13.lists
  1.4 0.0 copy-start
  1.4 0.5 collective-permute-start
  1.8 50.5 %exchange.1 = (bf16[144,12288]{1,0:T(8,128)(2,1)}, bf16[4096,128]{1,0:T(8,128)(2,1)}, bf16[64,256]{1,0:T(8,128)(2,1)}) custom-call(bf16[64,4096]{1,0:T(8,128)(2,1)} %points_ref.1, s32[1,4096]{1,0:T(1,128)} %bitcast.2, f32[64,4096]{1,0:T(8,128)} %direction.3, bf16[256,4096]{1,0:T(8,128)(2,1)} %basis.1, f32[5,256,256]{2,1,0:T(8,128)} %transfers_hbm.1, ...), custom_call_target="tpu_custom_call" | custom-call | flops 2147483648 | bytes 10485760 | tf_op jit(solution)/shard_map/exchange/pallas_call | solution.py:228
  52.3 0.0 copy-done
  52.3 0.0 collective-permute-done.before
  52.3 0.0 copy-start.1
  52.3 0.6 copy-done.1
  52.9 31.3 %near.1 = (f32[64,4096]{1,0:T(8,128)}, f32[4,64,128]{2,1,0:T(8,128)}) custom-call(s32[8,4]{1,0:T(8,128)} %copy-done, s32[8,4]{1,0:T(8,128)} %copy-done.1, s32[1]{0:T(128)} %bitcast.first_ref, bf16[4096,128]{1,0:T(8,128)(2,1)} %get-tuple-element.8.turned, bf16[144,12288]{1,0:T(8,128)(2,1)} %get-tuple-element.9.window, ...), custom_call_target="tpu_custom_call" | custom-call | tf_op jit(solution)/shard_map/near/pallas_call | solution.py:338
  84.2 17.2 %reduce.1.factors = f32[64,128]{1,0:T(8,128)} custom-call(f32[4,64,128]{2,1,0:T(8,128)} %get-tuple-element.11.sums_ref), custom_call_target="tpu_custom_call" | custom-call | tf_op jit(solution)/shard_map/reduce/pallas_call | solution.py:425
  101.4 4.5 %update.1 = (f32[64,4096]{1,0:T(8,128)}, f32[64,4096]{1,0:T(8,128)}, f32[64,4096]{1,0:T(8,128)}) custom-call(f32[64,128]{1,0:T(8,128)} %reduce.1.factors, f32[64,4096]{1,0:T(8,128)} %solution.1, f32[64,4096]{1,0:T(8,128)} %residual.3, f32[64,4096]{1,0:T(8,128)} %direction.3, f32[64,4096]{1,0:T(8,128)} %get-tuple-element.12.image), custom_call_target="tpu_custom_call" | custom-call | tf_op jit(solution)/shard_map/update/pallas_call | solution.py:461
Async XLA Ops:
  1.4 50.9 %copy-start = (s32[8,4]{1,0:T(8,128)}, s32[8,4]{1,0:T(8,128)S(1)}, u32[]{:S(2)}) copy-start(s32[8,4]{1,0:T(8,128)S(1)} %copy.13.lists) | copy-start | bytes 388
  1.4 50.9 %collective-permute-start = (s32[8,4]{1,0:T(8,128)S(1)}, s32[8,4]{1,0:T(8,128)S(1)}, u32[]{:S(2)}, u32[]{:S(2)}) collective-permute-start(s32[8,4]{1,0:T(8,128)S(1)} %copy.13.lists), channel_id=1, source_target_pairs={{0,1},{1,2},{2,3},{3,4},{4,5},{5,6},{6,7},{7,8},{8,9},{9,10},{10,1... | collective-permute-start | bytes 392 | tf_op jit(solution)/shard_map/ppermute | solution.py:23
  52.3 0.6 copy-start.1
